TPU v7x, 256 devices: a whole 4x4x8 slice. The times are simulated.
256 devices in a mesh: gx: 64 (over y, z, x_lo), gy: 4 (over x_hi, core).
Axes of the slice: x: 4 (x_hi: 2, x_lo: 2; x = x_hi * 2 + x_lo), y: 4, z: 8, core: 2. Of those that a mesh axis runs over, the one named last changes fastest.
Arguments:
- features: bfloat16 [524288, 128], P(('gx', 'gy')), may hold values from -6 to 6
- cotangent: bfloat16 [524288, 128], P(('gx', 'gy')), may hold values from -6 to 6
- kernel: bfloat16 [27, 128, 128], replicated, may hold values from -0.109375 to 0.109375
- block_count: int32 [256], P(('gx', 'gy')), may hold values from 8 to 32, as said below
- neighbours: int32 [8192, 27], P(('gx', 'gy')), may hold values from 0 to 72, as said below
- send_face: int32 [256, 4, 8], P(('gx', 'gy')), may hold values from 0 to 31, as said below
- send_corner: int32 [256, 4, 2], P(('gx', 'gy')), may hold values from 0 to 31, as said below
Outputs:
- conv_out: bfloat16 [524288, 128], P(('gx', 'gy'))
- input_grad: bfloat16 [524288, 128], P(('gx', 'gy'))
- kernel_grad: float32 [27, 128, 128], replicated
Inputs may be any that keep to these rules, and one draw needn't show every extreme that they name: `block_count`: live blocks of each device; in every draw some device has all 32 live. `neighbours`: entries index the device's extended table (own blocks 0 to 31, the zero block 32, then the face and corner blocks in the order of the steps). Entry 13 of a live block names the block itself; every entry of a block at or past the device's block count is 32; an own block that is named is live. A face block from x-1 (x+1) is named only at offsets with ox = -1 (+1), one from y-1 (y+1) only where oy = -1 (+1), a corner block only where (ox, oy) is its corner. `send_face`: each list holds 8 distinct live blocks of its device. `send_corner`: each list holds 2 distinct live blocks of its device.
All inputs are finite; a program needn't handle non-finite values.
Results may differ from a plain program's by a relative error of at most 0.0025.
Values may be sent and summed in bfloat16 or wider, within the bound.
A program may use at most 64 MiB of HBM per device.

v0:
```python
import math

import jax
import jax.numpy as jnp
from jax import lax
from jax.experimental import pallas as pl
from jax.experimental.pallas import tpu as pltpu
from jax.sharding import PartitionSpec as P

MESH = pl.DeviceIdType.MESH
BF = jnp.bfloat16
F32 = jnp.float32

NX, NY, NZ = 4, 4, 8
FACE_WAYS = ((-1, 0), (1, 0), (0, -1), (0, 1))
CORNER_WAYS = ((-1, -1), (-1, 1), (1, -1), (1, 1))
WAYS = FACE_WAYS + CORNER_WAYS


def opposite(channel):
    return channel ^ 1 if channel < 4 else 11 - channel


def side(stride):
    return 0 if stride < 0 else 3


def places(local):
    if local == 0:
        return ((1, 0), (5, 1))
    if local == 3:
        return ((4, 0), (0, -1))
    return ((local + 1, 0),)


def kind(local):
    return 0 if local == 0 else (2 if local == 3 else 1)


def readers(ux, uy, uz):
    found = []
    for px, ox in places(ux):
        for py, oy in places(uy):
            for pz, oz in places(uz):
                found.append((px, py, pz, (ox + 1) * 9 + (oy + 1) * 3 + oz + 1))
    return found


def nn(a, b):
    return lax.dot_general(a, b, (((1,), (0,)), ((), ())), preferred_element_type=F32)


def nt(a, b):
    return lax.dot_general(a, b, (((1,), (1,)), ((), ())), preferred_element_type=F32)


def onehot(mask):
    return jnp.where(mask, 1.0, 0.0).astype(BF)


def iota(shape, dim):
    return lax.broadcasted_iota(jnp.int32, shape, dim)


def body(
    cnt, feat, cot, ker, tab,
    conv, igrad, kgrad,
    et, pz, gz, gt, wt, dp, de, oh, oht, bd, bdt, perm,
    hs, hr, rs, rr,
    wd, rcore, hh, r1, s1, r2, s2, r3, tt, g3, g2,
    hsem, hrem, bsem, brem, csem, crem, asem, arem, lsem,
):
    gx = lax.axis_index("gx")
    gy = lax.axis_index("gy")
    cy = gx // 16
    cz = (gx // 2) % 8
    cx = (gy // 2) * 2 + gx % 2
    core = gy % 2

    def at(x, y, z, c):
        return ((y * 8 + z) * 2 + x % 2, (x // 2) * 2 + c)

    sibling = (gx, gy // 2 * 2 + (1 - core))
    along_x = [at((cx + d) % NX, cy, cz, core) for d in range(1, NX)]
    along_y = [at(cx, (cy + d) % NY, cz, core) for d in range(1, NY)]
    along_z = [at(cx, cy, (cz + d) % NZ, core) for d in range(1, NZ)]
    halo = [(gx + wx, gy + wy) for wx, wy in WAYS]
    there = [
        (gx + wx >= 0) & (gx + wx < 64) & (gy + wy >= 0) & (gy + wy < 4) for wx, wy in WAYS
    ]

    barrier = pltpu.get_barrier_semaphore()
    greet = [sibling] + along_x + along_y + along_z
    greet += [((gx + wx + 64) % 64, (gy + wy + 4) % 4) for wx, wy in WAYS]
    for other in greet:
        pl.semaphore_signal(barrier, inc=1, device_id=other, device_id_type=MESH)

    r256, c256 = iota((256, 256), 0), iota((256, 256), 1)
    perm[...] = onehot(((r256 >> 4) == (c256 & 15)) & ((r256 & 15) == (c256 >> 4)))
    eye = onehot(iota((128, 128), 0) == iota((128, 128), 1))
    eye256 = onehot(r256 == c256)

    def swap16(v):
        return nn(perm[...], v.reshape(256, 128)).reshape(16, 16, 128)

    for hb in range(2):
        for ug in range(4):
            rows = swap16(feat[pl.ds(16 * hb, 16), pl.ds(16 * ug, 16), :])
            et[pl.ds(16 * ug, 16), pl.ds(16 * hb, 16), :] = rows.astype(BF)

    r32, c32 = iota((32, 128), 0), iota((32, 128), 1)
    same_z = (r32 >> 3) == (c32 >> 5)
    for ch in range(8):
        pick = onehot(same_z & (tab[:, 27 + ch : 28 + ch] == (c32 & 31)))
        bd[ch] = pick
        bdt[ch] = nt(eye, pick).astype(BF)

    def rim_base(ch, chunk):
        wx, wy = WAYS[ch]
        ux = side(wx) if wx != 0 else chunk
        uy = side(wy) if wy != 0 else chunk
        return ux * 16 + uy * 4

    def chunks(ch):
        return 4 if ch < 4 else 1

    for ch in range(8):
        for chunk in range(chunks(ch)):
            source = et[pl.ds(rim_base(ch, chunk), 4), pl.ds(0, 32), :].reshape(128, 128)
            hs[ch, chunk] = nn(bd[ch], source).astype(BF)

    pl.semaphore_wait(barrier, len(greet))

    def part(buf, ch):
        return buf.at[ch] if ch < 4 else buf.at[ch, pl.ds(0, 1)]

    def halo_copy(src, dst, ss, rs_, ch):
        return pltpu.make_async_remote_copy(
            src_ref=part(src, ch),
            dst_ref=part(dst, opposite(ch)),
            send_sem=ss.at[ch],
            recv_sem=rs_.at[opposite(ch)],
            device_id=halo[ch],
            device_id_type=MESH,
        )

    def halo_arrived(src, dst, ss, rs_, ch):
        return pltpu.make_async_remote_copy(
            src_ref=part(src, ch),
            dst_ref=part(dst, ch),
            send_sem=ss.at[ch],
            recv_sem=rs_.at[ch],
            device_id=halo[ch],
            device_id_type=MESH,
        )

    for ch in range(8):
        @pl.when(there[ch])
        def _():
            halo_copy(hs, hr, hsem, hrem, ch).start()

    for x in range(4):
        for hb in range(2):
            live = jnp.where(iota((16, 128), 0) + 16 * hb < cnt[0], 1.0, 0.0)
            rows = swap16(cot[pl.ds(16 * hb, 16), pl.ds(16 * x, 16), :]) * live[None]
            rows = rows.reshape(4, 2, 2, 16, 128).astype(BF)
            gz[x, :, :, pl.ds(16 * hb, 16), pl.ds(0, 128)] = rows[:, :, 0]
            gz[x, :, :, pl.ds(16 * hb, 16), pl.ds(128, 128)] = rows[:, :, 1]
        gt[:, pl.ds(256 * x, 256)] = nt(eye256, gz[x].reshape(256, 256)).astype(BF)

    def weights(j, carry):
        low, mid, high = ker[3 * j], ker[3 * j + 1], ker[3 * j + 2]
        none = jnp.zeros((128, 128), BF)
        wt[j, 0, pl.ds(0, 128), pl.ds(0, 128)] = low
        wt[j, 0, pl.ds(0, 128), pl.ds(128, 128)] = none
        wt[j, 0, pl.ds(128, 128), pl.ds(0, 128)] = mid
        wt[j, 0, pl.ds(128, 128), pl.ds(128, 128)] = low
        wt[j, 1, pl.ds(0, 128), pl.ds(0, 128)] = high
        wt[j, 1, pl.ds(0, 128), pl.ds(128, 128)] = mid
        wt[j, 1, pl.ds(128, 128), pl.ds(0, 128)] = none
        wt[j, 1, pl.ds(128, 128), pl.ds(128, 128)] = high
        return carry

    lax.fori_loop(0, 9, weights, 0)

    columns = c32 + jnp.where(c32 >= 32, 1, 0)
    for o in range(27):
        oh[o] = onehot(tab[:, o : o + 1] == columns)

    def offsets_of(tx, ty, tz):
        pick = (0, 1, 3)
        return [r[3] for r in readers(pick[tx], pick[ty], pick[tz])]

    def stacked(offsets):
        if len(offsets) == 1:
            return oh[offsets[0]]
        return jnp.concatenate([oh[o] for o in offsets], axis=0)

    for tx in range(3):
        for ty in range(3):
            for tz in range(3):
                offs = offsets_of(tx, ty, tz)
                flipped = nt(eye[:80], stacked(offs)).astype(BF)
                oht[tx * 9 + ty * 3 + tz, :, pl.ds(0, 32 * len(offs))] = flipped

    def clear(u, carry):
        et[u, pl.ds(32, 96), :] = jnp.zeros((96, 128), BF)
        return carry

    lax.fori_loop(0, 64, clear, 0)

    def clear_dp(x, carry):
        dp[x] = jnp.zeros((6, 3, 32, 256), F32)
        return carry

    lax.fori_loop(0, 6, clear_dp, 0)

    def back(j, carry):
        kx = j // 3
        ky = j % 3
        for x in range(4):
            g = gz[x].reshape(256, 256)
            for w in range(2):
                term = nt(g, wt[j, w]).reshape(4, 2, 32, 256)
                dp[x + kx, pl.ds(ky, 4), pl.ds(w, 2)] += term
        return carry

    lax.fori_loop(0, 9, back, 0)

    for ch in range(8):
        @pl.when(there[ch])
        def _():
            halo_arrived(hs, hr, hsem, hrem, ch).wait_recv()
            wx, wy = WAYS[ch]
            for chunk in range(chunks(ch)):
                ux = side(-wx) if wx != 0 else chunk
                uy = side(-wy) if wy != 0 else chunk
                got = hr[ch, chunk].astype(F32).reshape(4, 8, 128)
                none = jnp.zeros((4, 8, 128), F32)
                pair = (got, none) if ch >= 4 or ch % 2 == 0 else (none, got)
                start = 64 if ch >= 4 else 32 + 16 * (ch // 2)
                et[pl.ds(ux * 16 + uy * 4, 4), pl.ds(start, 16), :] = jnp.concatenate(
                    pair, axis=1
                ).astype(BF)

    for ux in range(4):
        for uy in range(4):
            for uz in range(4):
                found = readers(ux, uy, uz)
                rows = nn(stacked([r[3] for r in found]), et[ux * 16 + uy * 4 + uz]).astype(BF)
                for n, (px, py, p, _) in enumerate(found):
                    pz[px, py, p // 2, :, pl.ds(128 * (p % 2), 128)] = rows[32 * n : 32 * n + 32]

    mine = pl.multiple_of(64 * core, 64)
    other = pl.multiple_of(64 - 64 * core, 64)

    def core_copy(s):
        return pltpu.make_async_remote_copy(
            src_ref=wd.at[pl.ds(9 * s, 9), pl.ds(other, 64), :],
            dst_ref=rcore.at[pl.ds(9 * s, 9)],
            send_sem=csem.at[s],
            recv_sem=crem.at[s],
            device_id=sibling,
            device_id_type=MESH,
        )

    for s in range(3):
        def slab(ky, carry):
            j = 3 * s + ky
            d0 = nn(gt[...], pz[pl.ds(s, 4), pl.ds(ky, 4), pl.ds(0, 2)].reshape(1024, 256))
            d1 = nn(gt[...], pz[pl.ds(s, 4), pl.ds(ky, 4), pl.ds(1, 2)].reshape(1024, 256))
            wd[3 * j] = (d0[:128, :128] + d0[128:, 128:]).T
            wd[3 * j + 1] = (d0[:128, 128:] + d1[128:, :128]).T
            wd[3 * j + 2] = (d1[:128, :128] + d1[128:, 128:]).T
            return carry

        lax.fori_loop(0, 3, slab, 0)
        core_copy(s).start()

    def send(src, dst, n, device):
        return pltpu.make_async_remote_copy(
            src_ref=src,
            dst_ref=dst,
            send_sem=asem.at[n],
            recv_sem=arem.at[n],
            device_id=device,
            device_id_type=MESH,
        )

    for s in range(3):
        core_copy(s).wait()
        hh[pl.ds(9 * s, 9)] = wd[pl.ds(9 * s, 9), pl.ds(mine, 64), :] + rcore[pl.ds(9 * s, 9)]

    def at8(first, index):
        return pl.ds(pl.multiple_of(first + 8 * index, 8), 8)

    first = []
    for d in range(1, 4):
        first.append(send(hh.at[:, at8(0, (cx + d) % 4), :], r1.at[0, d - 1], d - 1, along_x[d - 1]))
        first.append(send(hh.at[:, at8(32, (cy + d) % 4), :], r1.at[1, d - 1], d + 2, along_y[d - 1]))
    for copy in first:
        copy.start()

    for x in range(4):
        total = jnp.zeros((256, 256), F32)
        for kx in range(3):
            for ky in range(3):
                for w in range(2):
                    rows = pz[x + kx, pl.ds(ky, 4), pl.ds(w, 2)].reshape(256, 256)
                    total = total + nn(rows, wt[3 * kx + ky, w])
        total = total.reshape(4, 2, 32, 256)
        for hb in range(2):
            live = jnp.where(iota((16, 128), 0) + 16 * hb < cnt[0], 1.0, 0.0)
            even = total[:, :, 16 * hb : 16 * hb + 16, :128] * live
            odd = total[:, :, 16 * hb : 16 * hb + 16, 128:] * live
            both = jnp.stack([even, odd], axis=2).astype(BF).reshape(16, 16, 128)
            conv[pl.ds(16 * hb, 16), pl.ds(16 * x, 16), :] = swap16(both).astype(BF)

    for copy in first:
        copy.wait()
    s1[0, pl.ds(0, 27)] = hh[:, at8(0, cx), :] + r1[0, 0] + r1[0, 1] + r1[0, 2]
    s1[1, pl.ds(0, 27)] = hh[:, at8(32, cy), :] + r1[1, 0] + r1[1, 1] + r1[1, 2]
    s1[:, pl.ds(27, 1)] = jnp.zeros((2, 1, 8, 128), F32)

    second = []
    for d in range(1, 4):
        second.append(send(s1.at[0, pl.ds(7 * ((cy + d) % 4), 7)], r2.at[0, d - 1], d + 5, along_y[d - 1]))
        second.append(send(s1.at[1, pl.ds(7 * ((cx + d) % 4), 7)], r2.at[1, d - 1], d + 8, along_x[d - 1]))
    for copy in second:
        copy.start()

    for ux in range(4):
        for uy in range(4):
            pieces = []
            for uz in range(4):
                found = readers(ux, uy, uz)
                high, low = [], []
                for px, py, p, _ in found:
                    value = dp[px, py, p // 2, :, pl.ds(128 * (p % 2), 128)]
                    top = value.astype(BF)
                    high.append(top)
                    low.append((value - top.astype(F32)).astype(BF))
                high = jnp.concatenate(high, axis=0) if len(high) > 1 else high[0]
                low = jnp.concatenate(low, axis=0) if len(low) > 1 else low[0]
                group = kind(ux) * 9 + kind(uy) * 3 + kind(uz)
                res = nn(
                    oht[group, :, pl.ds(0, 32 * len(found))],
                    jnp.concatenate([high, low], axis=1),
                )
                res = res[:, :128] + res[:, 128:]
                de[ux * 16 + uy * 4 + uz] = res[:32]
                pieces.append(res)

            def give(slot, chunk, row):
                rs[slot, chunk] = jnp.concatenate(
                    [piece[row : row + 8] for piece in pieces], axis=0
                ).astype(BF)

            for slot in range(8):
                wx, wy = WAYS[slot]
                if (wx != 0 and ux != side(-wx)) or (wy != 0 and uy != side(-wy)):
                    continue
                chunk = 0 if slot >= 4 else (uy if wx != 0 else ux)
                give(slot, chunk, 64 if slot >= 4 else 32 + 8 * slot)

    for ch in range(8):
        @pl.when(there[ch])
        def _():
            halo_copy(rs, rr, bsem, brem, ch).start()

        @pl.when(jnp.logical_not(there[ch]))
        def _():
            rr[ch] = jnp.zeros((4, 32, 128), BF)

    for copy in second:
        copy.wait()
    s2[0, pl.ds(0, 7)] = s1[0, pl.ds(7 * cy, 7)] + r2[0, 0] + r2[0, 1] + r2[0, 2]
    s2[1, pl.ds(0, 7)] = s1[1, pl.ds(7 * cx, 7)] + r2[1, 0] + r2[1, 1] + r2[1, 2]
    s2[:, pl.ds(7, 1)] = jnp.zeros((2, 1, 8, 128), F32)

    third = [
        send(s2.at[:, pl.ds((cz + d) % 8, 1)], r3.at[d - 1], 11 + d, along_z[d - 1])
        for d in range(1, 8)
    ]
    for copy in third:
        copy.start()
    for copy in third:
        copy.wait()
    whole = s2[:, pl.ds(cz, 1)]
    for d in range(7):
        whole = whole + r3[d]
    tt[...] = whole * (1.0 / math.sqrt(256 * 32 * 64))
    g3[:, pl.ds(cz, 1)] = tt[...]

    fourth = [send(tt, g3.at[:, pl.ds(cz, 1)], 18 + d, along_z[d - 1]) for d in range(1, 8)]
    for copy in fourth:
        copy.start()

    for ch in range(8):
        @pl.when(there[ch])
        def _():
            halo_arrived(rs, rr, bsem, brem, ch).wait_recv()

    for ux in range(4):
        parts = []
        for uy in range(4):
            rows = de[pl.ds(ux * 16 + uy * 4, 4)].reshape(128, 128)
            for ch in range(8):
                wx, wy = WAYS[ch]
                if (wx != 0 and ux != side(wx)) or (wy != 0 and uy != side(wy)):
                    continue
                chunk = 0 if ch >= 4 else (uy if wx != 0 else ux)
                rows = rows + nn(bdt[ch], rr[ch, chunk])
            parts.append(rows.astype(BF).reshape(4, 32, 128))
        parts = jnp.concatenate(parts, axis=0)
        for hb in range(2):
            swapped = swap16(parts[:, 16 * hb : 16 * hb + 16])
            igrad[pl.ds(16 * hb, 16), pl.ds(16 * ux, 16), :] = swapped.astype(BF)

    for copy in fourth:
        copy.wait()
    g2[0, pl.ds(7 * cy, 7)] = g3[0, pl.ds(0, 7)]
    g2[1, pl.ds(7 * cx, 7)] = g3[1, pl.ds(0, 7)]
    fifth = []
    for d in range(1, 4):
        fifth.append(send(g3.at[0, pl.ds(0, 7)], g2.at[0, pl.ds(7 * cy, 7)], 25 + d, along_y[d - 1]))
        fifth.append(send(g3.at[1, pl.ds(0, 7)], g2.at[1, pl.ds(7 * cx, 7)], 28 + d, along_x[d - 1]))
    for copy in fifth:
        copy.start()
    for copy in fifth:
        copy.wait()

    def rows_of(base, x):
        return pl.ds(pl.multiple_of(64 * core + base + 8 * x, 8), 8)

    sixth = []
    for d in range(1, 4):
        sixth.append(send(g2.at[0, pl.ds(0, 27)], kgrad.at[:, rows_of(0, cx), :], 31 + d, along_x[d - 1]))
        sixth.append(send(g2.at[1, pl.ds(0, 27)], kgrad.at[:, rows_of(32, cy), :], 34 + d, along_y[d - 1]))
    for copy in sixth:
        copy.start()
    own = []
    for n, (base, index) in enumerate(((0, cx), (32, cy))):
        rows = kgrad.at[:, rows_of(base, index), :]
        local = pltpu.make_async_copy(g2.at[n, pl.ds(0, 27)], rows, lsem.at[n])
        local.start()
        own.append(local)
        twin = send(g2.at[n, pl.ds(0, 27)], rows, 38 + n, sibling)
        twin.start()
        own.append(twin)
    last = []
    for n in range(6):
        sixth[n].wait()
        d = n // 2 + 1
        base, index = ((0, (cx + 4 - d) % 4), (32, (cy + 4 - d) % 4))[n % 2]
        rows = kgrad.at[:, rows_of(base, index), :]
        forward = send(rows, rows, 40 + n, sibling)
        forward.start()
        last.append(forward)
    for copy in own + last:
        copy.wait()

    for ch in range(8):
        @pl.when(there[ch])
        def _():
            halo_copy(hs, hr, hsem, hrem, ch).wait_send()
            halo_copy(rs, rr, bsem, brem, ch).wait_send()


def per_device(features, cotangent, kernel, block_count, neighbours, send_face, send_corner):
    face = jnp.tile(send_face[0].T, (4, 1))
    slot = jnp.arange(8)[:, None] // 2 == 3 - jnp.arange(4)[None, :]
    corner = jnp.where(slot, jnp.tile(send_corner[0].T, (4, 1)), -1)
    table = jnp.concatenate([neighbours, face, jnp.tile(corner, (4, 1))], axis=1)
    vmem = pl.BlockSpec(memory_space=pltpu.VMEM)
    dma = pltpu.SemaphoreType.DMA
    conv, igrad, kgrad = pl.pallas_call(
        body,
        out_shape=(
            jax.ShapeDtypeStruct((32, 64, 128), BF),
            jax.ShapeDtypeStruct((32, 64, 128), BF),
            jax.ShapeDtypeStruct((27, 128, 128), F32),
        ),
        in_specs=[pl.BlockSpec(memory_space=pltpu.SMEM)] + [vmem] * 4,
        out_specs=(vmem, vmem, pl.BlockSpec(memory_space=pl.ANY)),
        scratch_shapes=[
            pltpu.VMEM((64, 128, 128), BF),
            pltpu.VMEM((6, 6, 3, 32, 256), BF),
            pltpu.VMEM((4, 4, 2, 32, 256), BF),
            pltpu.VMEM((256, 1024), BF),
            pltpu.VMEM((9, 2, 256, 256), BF),
            pltpu.VMEM((6, 6, 3, 32, 256), F32),
            pltpu.VMEM((64, 32, 128), F32),
            pltpu.VMEM((27, 32, 128), BF),
            pltpu.VMEM((27, 80, 256), BF),
            pltpu.VMEM((8, 32, 128), BF),
            pltpu.VMEM((8, 128, 32), BF),
            pltpu.VMEM((256, 256), BF),
            pltpu.VMEM((8, 4, 32, 128), BF),
            pltpu.VMEM((8, 4, 32, 128), BF),
            pltpu.VMEM((8, 4, 32, 128), BF),
            pltpu.VMEM((8, 4, 32, 128), BF),
            pltpu.VMEM((27, 128, 128), F32),
            pltpu.VMEM((27, 64, 128), F32),
            pltpu.VMEM((27, 64, 128), F32),
            pltpu.VMEM((2, 3, 27, 8, 128), F32),
            pltpu.VMEM((2, 28, 8, 128), F32),
            pltpu.VMEM((2, 3, 7, 8, 128), F32),
            pltpu.VMEM((2, 8, 8, 128), F32),
            pltpu.VMEM((7, 2, 1, 8, 128), F32),
            pltpu.VMEM((2, 1, 8, 128), F32),
            pltpu.VMEM((2, 8, 8, 128), F32),
            pltpu.VMEM((2, 28, 8, 128), F32),
            dma((8,)), dma((8,)), dma((8,)), dma((8,)),
            dma((3,)), dma((3,)), dma((46,)), dma((46,)), dma((2,)),
        ],
        compiler_params=pltpu.CompilerParams(
            collective_id=0, has_side_effects=True, vmem_limit_bytes=48 * 1024 * 1024
        ),
        cost_estimate=pl.CostEstimate(
            flops=7_000_000_000, bytes_accessed=6_000_000, transcendentals=0
        ),
    )(
        block_count,
        features.reshape(32, 64, 128),
        cotangent.reshape(32, 64, 128),
        kernel,
        table,
    )
    return conv.reshape(2048, 128), igrad.reshape(2048, 128), kgrad


def solution(mesh):
    in_specs = (
        P(("gx", "gy"), None),
        P(("gx", "gy"), None),
        P(),
        P(("gx", "gy")),
        P(("gx", "gy"), None),
        P(("gx", "gy"), None, None),
        P(("gx", "gy"), None, None),
    )
    out_specs = (P(("gx", "gy"), None), P(("gx", "gy"), None), P())
    return jax.shard_map(
        per_device, mesh=mesh, in_specs=in_specs, out_specs=out_specs, check_vma=False
    )
```

profile of v0, /device:TPU:1, one launch (start us, length us, event | category | flops | bytes accessed | tf_op | source)
XLA Modules:
  0.0 71.5 jit_solution(7886386122677036395)
XLA Ops:
  1.3 0.8 %copy.15 = s32[8,4]{1,0:T(8,128)S(1)} copy(s32[8,4]{0,1:T(4,128)} %bitcast.20) | data formatting | bytes 256
  2.1 0.7 tile.14
  2.7 0.1 compare_select_fusion
  2.8 0.8 %pad_add_fusion.tab = s32[32,35]{1,0:T(8,128)S(1)} fusion(s32[32,4]{1,0:T(8,128)S(1)} %get-tuple-element.9, s32[32,4]{1,0:T(8,128)S(1)} %get-tuple-element.10, s32[32,27]{1,0:T(8,128)} %param.11), kind=kLoop, calls=%fused_computation | loop fusion | flops 2240 | bytes 8960 | tf_op jit(solution)/shard_map/concatenate | solution.py:474
  3.6 0.0 copy-start
  3.6 1.2 %copy-done = bf16[27,128,128]{2,1,0:T(8,128)(2,1)S(1)} copy-done((bf16[27,128,128]{2,1,0:T(8,128)(2,1)S(1)}, bf16[27,128,128]{2,1,0:T(8,128)(2,1)}, u32[]{:S(2)}) %copy-start) | copy-done | bytes 884760
  4.8 0.0 copy-start.1
  4.8 1.0 %copy-done.1 = bf16[2048,128]{1,0:T(8,128)(2,1)S(1)} copy-done((bf16[2048,128]{1,0:T(8,128)(2,1)S(1)}, bf16[2048,128]{1,0:T(8,128)(2,1)}, u32[]{:S(2)}) %copy-start.1) | copy-done | bytes 524312
  5.8 0.0 copy-start.2
  5.8 1.0 %copy-done.2 = bf16[2048,128]{1,0:T(8,128)(2,1)S(1)} copy-done((bf16[2048,128]{1,0:T(8,128)(2,1)S(1)}, bf16[2048,128]{1,0:T(8,128)(2,1)}, u32[]{:S(2)}) %copy-start.2) | copy-done | bytes 524312
  6.9 61.9 %shard_map.94 = (bf16[32,64,128]{2,1,0:T(8,128)(2,1)S(1)}, bf16[32,64,128]{2,1,0:T(8,128)(2,1)S(1)}, f32[27,128,128]{2,1,0:T(8,128)S(1)}) custom-call(s32[1]{0:T(128)S(6)} %copy.20.cnt, bf16[32,64,128]{2,1,0:T(8,128)(2,1)S(1)} %bitcast.17, bf16[32,64,128]{2,1,0:T(8,128)(2,1)S(1)} %bitcast.18, bf16[27,128,128]{2,1,0:T(8,128)(2,1)S(1)} %copy-done, ...), custom_call_target="tpu_custom_call" | custom-call | flops 7000000000 | bytes 6000000 | tf_op jit(solution)/shard_map/pallas_call | solution.py:477
  68.7 0.8 %copy.21 = bf16[2048,128]{1,0:T(8,128)(2,1)} copy(bf16[2048,128]{1,0:T(8,128)(2,1)S(1)} %bitcast.16) | data formatting | bytes 1048576
  69.5 0.8 %copy.22 = bf16[2048,128]{1,0:T(8,128)(2,1)} copy(bf16[2048,128]{1,0:T(8,128)(2,1)S(1)} %bitcast.15) | data formatting | bytes 1048576
  70.3 1.2 %copy.23 = f32[27,128,128]{2,1,0:T(8,128)} copy(f32[27,128,128]{2,1,0:T(8,128)S(1)} %get-tuple-element.16) | data formatting | bytes 3538944
  (3 shorter events, 0.0 us)
Async XLA Ops:
  3.6 1.2 %copy-start = (bf16[27,128,128]{2,1,0:T(8,128)(2,1)S(1)}, bf16[27,128,128]{2,1,0:T(8,128)(2,1)}, u32[]{:S(2)}) copy-start(bf16[27,128,128]{2,1,0:T(8,128)(2,1)} %ker.1) | copy-start | bytes 2654212
  4.8 1.0 %copy-start.1 = (bf16[2048,128]{1,0:T(8,128)(2,1)S(1)}, bf16[2048,128]{1,0:T(8,128)(2,1)}, u32[]{:S(2)}) copy-start(bf16[2048,128]{1,0:T(8,128)(2,1)} %param.7) | copy-start | bytes 1572868
  5.8 1.0 %copy-start.2 = (bf16[2048,128]{1,0:T(8,128)(2,1)S(1)}, bf16[2048,128]{1,0:T(8,128)(2,1)}, u32[]{:S(2)}) copy-start(bf16[2048,128]{1,0:T(8,128)(2,1)} %param.8) | copy-start | bytes 1572868
where the time goes:
time: 71.9 us; the launch traced here: 71.5 us
  Pallas kernels  61.9 us (86%)
  local copies, waits for them, and re-layouts  7.49 us (10%)
  between operations  1.31 us (2%)
  other arithmetic  0.87 us (1%)
    pallas_call x1, Pallas kernels, per_device(): pl.pallas_call(body, out_shape=(jax.ShapeDtypeStruct((32, 64, 128), BF),...  61.9 us
    unnamed x10, local copies, waits for them, and re-layouts  6.81 us

commit v1 on v0

v1 whole, which is shorter than its diff:
```python
import math

import jax
import jax.numpy as jnp
from jax import lax
from jax.experimental import pallas as pl
from jax.experimental.pallas import tpu as pltpu
from jax.sharding import PartitionSpec as P

MESH = pl.DeviceIdType.MESH
BF = jnp.bfloat16
F32 = jnp.float32

NX, NY, NZ = 4, 4, 8
FACE_WAYS = ((-1, 0), (1, 0), (0, -1), (0, 1))
CORNER_WAYS = ((-1, -1), (-1, 1), (1, -1), (1, 1))
WAYS = FACE_WAYS + CORNER_WAYS


RUNS = (
    ((0, 0, 5), (5, 0, 4)),
    ((9, 5, 4), (13, 4, 5)),
    ((18, 9, 5), (23, 9, 4)),
)


def opposite(channel):
    return channel ^ 1 if channel < 4 else 11 - channel


def side(stride):
    return 0 if stride < 0 else 3


def places(local):
    if local == 0:
        return ((1, 0), (5, 1))
    if local == 3:
        return ((4, 0), (0, -1))
    return ((local + 1, 0),)


def kind(local):
    return 0 if local == 0 else (2 if local == 3 else 1)


def readers(ux, uy, uz):
    found = []
    for px, ox in places(ux):
        for py, oy in places(uy):
            for pz, oz in places(uz):
                found.append((px, py, pz, (ox + 1) * 9 + (oy + 1) * 3 + oz + 1))
    return found


def nn(a, b):
    return lax.dot_general(a, b, (((1,), (0,)), ((), ())), preferred_element_type=F32)


def nt(a, b):
    return lax.dot_general(a, b, (((1,), (1,)), ((), ())), preferred_element_type=F32)


def onehot(mask):
    return jnp.where(mask, 1.0, 0.0).astype(BF)


def iota(shape, dim):
    return lax.broadcasted_iota(jnp.int32, shape, dim)


def body(
    cnt, face, corner, feat_in, cot_in, ker_in, near_in,
    conv_out, igrad_out, kg,
    feat, cot, ker, near, conv, igrad,
    et, pz, gz, gt, gty, wt, di, dp, de, oh, oht, bd, bdt, co, perm, pair_perm, part_perm,
    hs, hr, rs, rr,
    wd, rcore, hh, r1, s1, r2, s2, r3, tt, g3, g2,
    isem, osem, hsem, hrem, bsem, brem, csem, crem, asem, arem,
):
    loads = [
        pltpu.make_async_copy(src, dst, isem.at[n])
        for n, (src, dst) in enumerate(
            ((feat_in, feat), (cot_in, cot), (near_in, near), (ker_in, ker))
        )
    ]
    for copy in loads:
        copy.start()
    gx = lax.axis_index("gx")
    gy = lax.axis_index("gy")
    cy = gx // 16
    cz = (gx // 2) % 8
    cx = (gy // 2) * 2 + gx % 2
    core = gy % 2

    def at(x, y, z, c):
        return ((y * 8 + z) * 2 + x % 2, (x // 2) * 2 + c)

    sibling = (gx, gy // 2 * 2 + (1 - core))
    along_x = [at((cx + d) % NX, cy, cz, core) for d in range(1, NX)]
    along_y = [at(cx, (cy + d) % NY, cz, core) for d in range(1, NY)]
    along_z = [at(cx, cy, (cz + d) % NZ, core) for d in range(1, NZ)]
    halo = [(gx + wx, gy + wy) for wx, wy in WAYS]
    there = [
        (gx + wx >= 0) & (gx + wx < 64) & (gy + wy >= 0) & (gy + wy < 4) for wx, wy in WAYS
    ]

    barrier = pltpu.get_barrier_semaphore()
    greet = [sibling] + along_x + along_y + along_z
    greet += [((gx + wx + 64) % 64, (gy + wy + 4) % 4) for wx, wy in WAYS]
    for other in greet:
        pl.semaphore_signal(barrier, inc=1, device_id=other, device_id_type=MESH)

    r256, c256 = iota((256, 256), 0), iota((256, 256), 1)
    perm[...] = onehot(((r256 >> 4) == (c256 & 15)) & ((r256 & 15) == (c256 >> 4)))
    pair_perm[...] = onehot(c256 == (r256 & 15) * 16 + ((r256 >> 4) & 7) * 2 + (r256 >> 7))
    part_perm[...] = onehot(c256 == (r256 & 1) * 128 + ((r256 & 15) >> 1) * 16 + (r256 >> 4))
    eye = onehot(iota((128, 128), 0) == iota((128, 128), 1))
    eye256 = onehot(r256 == c256)

    def swap16(v):
        return nn(perm[...], v.reshape(256, 128)).reshape(16, 16, 128)

    r32, c32 = iota((32, 128), 0), iota((32, 128), 1)
    same_z = (r32 >> 3) == (c32 >> 5)
    for ch in range(8):
        index = jnp.full((32, 128), -1, jnp.int32)
        for n in range(8 if ch < 4 else 2):
            slot = n if ch < 4 else 2 * (opposite(ch) - 4) + n
            block = face[0, ch, n] if ch < 4 else corner[0, n, ch - 4]
            index = jnp.where((r32 & 7) == slot, block, index)
        pick = onehot(same_z & (index == (c32 & 31)))
        bd[ch] = pick
        bdt[ch] = nt(eye, pick).astype(BF)

    loads[0].wait()
    for hb in range(2):
        for ug in range(4):
            rows = swap16(feat[pl.ds(16 * hb, 16), pl.ds(16 * ug, 16), :])
            et[pl.ds(16 * ug, 16), pl.ds(16 * hb, 16), :] = rows.astype(BF)

    def rim_base(ch, chunk):
        wx, wy = WAYS[ch]
        ux = side(wx) if wx != 0 else chunk
        uy = side(wy) if wy != 0 else chunk
        return ux * 16 + uy * 4

    def chunks(ch):
        return 4 if ch < 4 else 1

    for ch in range(8):
        for chunk in range(chunks(ch)):
            source = et[pl.ds(rim_base(ch, chunk), 4), pl.ds(0, 32), :].reshape(128, 128)
            hs[ch, chunk] = nn(bd[ch], source).astype(BF)

    pl.semaphore_wait(barrier, len(greet))

    def part(buf, ch):
        return buf.at[ch] if ch < 4 else buf.at[ch, pl.ds(0, 1)]

    def halo_copy(src, dst, ss, rs_, ch):
        return pltpu.make_async_remote_copy(
            src_ref=part(src, ch),
            dst_ref=part(dst, opposite(ch)),
            send_sem=ss.at[ch],
            recv_sem=rs_.at[opposite(ch)],
            device_id=halo[ch],
            device_id_type=MESH,
        )

    def halo_arrived(src, dst, ss, rs_, ch):
        return pltpu.make_async_remote_copy(
            src_ref=part(src, ch),
            dst_ref=part(dst, ch),
            send_sem=ss.at[ch],
            recv_sem=rs_.at[ch],
            device_id=halo[ch],
            device_id_type=MESH,
        )

    for ch in range(8):
        @pl.when(there[ch])
        def _():
            halo_copy(hs, hr, hsem, hrem, ch).start()

    lives = [jnp.where(iota((16, 128), 0) + 16 * hb < cnt[0], 1.0, 0.0) for hb in range(2)]
    loads[1].wait()
    for x in range(4):
        for hb in range(2):
            rows = cot[pl.ds(16 * hb, 16), pl.ds(16 * x, 16), :].reshape(256, 128)
            rows = nn(pair_perm[...], rows).reshape(2, 4, 2, 16, 128) * lives[hb]
            for n in range(2):
                gz[x, :, :, pl.ds(16 * hb, 16), pl.ds(128 * n, 128)] = rows[n].astype(BF)
        turned = nt(eye256, gz[x].reshape(256, 256))
        place = pl.ds(256 * x, 256)
        gt[0, :, place] = jnp.where(c256 < 64, 0.0, turned).astype(BF)
        gt[1, :, place] = turned.astype(BF)
        gt[2, :, place] = jnp.where(c256 < 192, turned, 0.0).astype(BF)
    for n, y in enumerate((0, 3)):
        gty[n] = nt(eye256, gz[:, y].reshape(256, 256)).astype(BF)

    loads[2].wait()
    columns = c32 + jnp.where(c32 >= 32, 1, 0)
    for o in range(27):
        oh[o] = onehot(near[:, o : o + 1] == columns)

    def offsets_of(tx, ty, tz):
        pick = (0, 1, 3)
        return [r[3] for r in readers(pick[tx], pick[ty], pick[tz])]

    def stacked(offsets):
        if len(offsets) == 1:
            return oh[offsets[0]]
        return jnp.concatenate([oh[o] for o in offsets], axis=0)

    def clear(u, carry):
        et[u, pl.ds(32, 96), :] = jnp.zeros((96, 128), BF)
        return carry

    lax.fori_loop(0, 64, clear, 0)

    def inner(found):
        return [r for r in found if 1 <= r[0] <= 4 and 1 <= r[1] <= 4]

    def outer(found):
        return [r for r in found if not (1 <= r[0] <= 4 and 1 <= r[1] <= 4)]

    def keep(rows, found):
        for n, (px, py, p, _) in enumerate(found):
            pz[px, py, p // 2, :, pl.ds(128 * (p % 2), 128)] = rows[32 * n : 32 * n + 32]

    for py in (0, 5):
        pz[pl.ds(1, 4), py] = jnp.zeros((4, 3, 32, 256), BF)
    for ux in range(4):
        for uy in range(4):
            for uz in range(4):
                found = inner(readers(ux, uy, uz))
                picks = stacked([r[3] for r in found])[:, :32]
                keep(nn(picks, et[ux * 16 + uy * 4 + uz, pl.ds(0, 32)]).astype(BF), found)

    def blocks_of(d0, d1):
        return (
            d0[:128, :128] + d0[128:, 128:],
            d0[:128, 128:] + d1[128:, :128],
            d1[:128, :128] + d1[128:, 128:],
        )

    for kx in range(3):
        x0, x1 = ((1, 4), (0, 4), (0, 3))[kx]
        for ky in range(3):
            left = gt[ky, :, pl.ds(256 * x0, 256 * (x1 - x0))]
            sums = [
                nn(
                    left,
                    pz[pl.ds(x0 + kx, x1 - x0), pl.ds(ky, 4), pl.ds(w, 2)].reshape(-1, 256),
                )
                for w in range(2)
            ]
            for n, value in enumerate(blocks_of(*sums)):
                if kx == 1 and ky == 1:
                    wd[9 * kx + 3 * ky + n] = value.T
                else:
                    di[9 * kx + 3 * ky + n] = value

    for ch in range(8):
        @pl.when(there[ch])
        def _():
            halo_arrived(hs, hr, hsem, hrem, ch).wait_recv()
            wx, wy = WAYS[ch]
            for chunk in range(chunks(ch)):
                ux = side(-wx) if wx != 0 else chunk
                uy = side(-wy) if wy != 0 else chunk
                got = hr[ch, chunk].astype(F32).reshape(4, 8, 128)
                none = jnp.zeros((4, 8, 128), F32)
                pair = (got, none) if ch >= 4 or ch % 2 == 0 else (none, got)
                start = 64 if ch >= 4 else 32 + 16 * (ch // 2)
                et[pl.ds(ux * 16 + uy * 4, 4), pl.ds(start, 16), :] = jnp.concatenate(
                    pair, axis=1
                ).astype(BF)

    for ux in range(4):
        for uy in range(4):
            for uz in range(4):
                found = outer(readers(ux, uy, uz))
                if found:
                    picks = stacked([r[3] for r in found])
                    keep(nn(picks, et[ux * 16 + uy * 4 + uz]).astype(BF), found)

    mine = pl.multiple_of(64 * core, 64)
    other = pl.multiple_of(64 - 64 * core, 64)

    def core_copy(s):
        return pltpu.make_async_remote_copy(
            src_ref=wd.at[pl.ds(9 * s, 9), pl.ds(other, 64), :],
            dst_ref=rcore.at[pl.ds(9 * s, 9)],
            send_sem=csem.at[s],
            recv_sem=crem.at[s],
            device_id=sibling,
            device_id_type=MESH,
        )

    def send(src, dst, n, device):
        return pltpu.make_async_remote_copy(
            src_ref=src,
            dst_ref=dst,
            send_sem=asem.at[n],
            recv_sem=arem.at[n],
            device_id=device,
            device_id_type=MESH,
        )

    def sixteen(first, index):
        return pl.ds(pl.multiple_of(first + 16 * index, 16), 16)

    def quarter(index):
        return pl.ds(4 * index, 4)

    first = []

    def core_sum(s):
        core_copy(s).wait()
        hh[pl.ds(9 * s, 9)] = wd[pl.ds(9 * s, 9), pl.ds(mine, 64), :] + rcore[pl.ds(9 * s, 9)]
        for n, (matrix, slot, count) in enumerate(RUNS[s]):
            for d in range(1, 4):
                place = (cx, cy)[n]
                copy = send(
                    hh.at[pl.ds(matrix, count), sixteen(0, (place + d) % 4), :],
                    r1.at[n, d - 1, pl.ds(slot, count)],
                    6 * s + 3 * n + d - 1,
                    (along_x, along_y)[n][d - 1],
                )
                copy.start()
                first.append(copy)

    def outer_sums(kx, ky, w):
        total = None
        if ky != 1:
            rows = pz[pl.ds(kx, 4), (0, None, 5)[ky], pl.ds(w, 2)].reshape(256, 256)
            total = nn(gty[ky // 2], rows)
        if kx != 1:
            x, px = ((0, 0), None, (3, 5))[kx]
            rows = pz[px, pl.ds(ky, 4), pl.ds(w, 2)].reshape(256, 256)
            term = nn(gt[ky, :, pl.ds(256 * x, 256)], rows)
            total = term if total is None else total + term
        return total

    for s in (1, 0, 2):
        for ky in range(3):
            if s == 1 and ky == 1:
                continue
            value = blocks_of(outer_sums(s, ky, 0), outer_sums(s, ky, 1))
            for n in range(3):
                j = 9 * s + 3 * ky + n
                wd[j] = (di[j] + value[n]).T
        core_copy(s).start()
    for s in (1, 0, 2):
        core_sum(s)

    def weights(j, carry):
        low, mid, high = ker[3 * j], ker[3 * j + 1], ker[3 * j + 2]
        none = jnp.zeros((128, 128), BF)
        wt[j, 0, pl.ds(0, 128), pl.ds(0, 128)] = low
        wt[j, 0, pl.ds(0, 128), pl.ds(128, 128)] = none
        wt[j, 0, pl.ds(128, 128), pl.ds(0, 128)] = mid
        wt[j, 0, pl.ds(128, 128), pl.ds(128, 128)] = low
        wt[j, 1, pl.ds(0, 128), pl.ds(0, 128)] = high
        wt[j, 1, pl.ds(0, 128), pl.ds(128, 128)] = mid
        wt[j, 1, pl.ds(128, 128), pl.ds(0, 128)] = none
        wt[j, 1, pl.ds(128, 128), pl.ds(128, 128)] = high
        return carry

    loads[3].wait()
    lax.fori_loop(0, 9, weights, 0)

    for tx in range(3):
        for ty in range(3):
            for tz in range(3):
                offs = offsets_of(tx, ty, tz)
                flipped = nt(eye[:80], stacked(offs)).astype(BF)
                oht[tx * 9 + ty * 3 + tz, :, pl.ds(0, 32 * len(offs))] = flipped

    def clear_dp(x, carry):
        dp[x] = jnp.zeros((6, 3, 32, 256), F32)
        return carry

    lax.fori_loop(0, 6, clear_dp, 0)

    for px in range(6):
        for ky in range(3):
            for w in range(2):
                term = None
                for kx in range(3):
                    if 0 <= px - kx < 4:
                        one = nt(gz[px - kx].reshape(256, 256), wt[3 * kx + ky, w])
                        term = one if term is None else term + one
                dp[px, pl.ds(ky, 4), pl.ds(w, 2)] += term.reshape(4, 2, 32, 256)

    for ux in range(4):
        for uy in range(4):
            pieces = []
            for uz in range(4):
                found = readers(ux, uy, uz)
                high, low = [], []
                for px, py, p, _ in found:
                    value = dp[px, py, p // 2, :, pl.ds(128 * (p % 2), 128)]
                    top = value.astype(BF)
                    high.append(top)
                    low.append((value - top.astype(F32)).astype(BF))
                high = jnp.concatenate(high, axis=0) if len(high) > 1 else high[0]
                low = jnp.concatenate(low, axis=0) if len(low) > 1 else low[0]
                group = kind(ux) * 9 + kind(uy) * 3 + kind(uz)
                res = nn(
                    oht[group, :, pl.ds(0, 32 * len(found))],
                    jnp.concatenate([high, low], axis=1),
                )
                res = res[:, :128] + res[:, 128:]
                de[ux * 16 + uy * 4 + uz] = res[:32]
                pieces.append(res)

            def give(slot, chunk, row):
                rs[slot, chunk] = jnp.concatenate(
                    [piece[row : row + 8] for piece in pieces], axis=0
                ).astype(BF)

            for slot in range(8):
                wx, wy = WAYS[slot]
                if (wx != 0 and ux != side(-wx)) or (wy != 0 and uy != side(-wy)):
                    continue
                chunk = 0 if slot >= 4 else (uy if wx != 0 else ux)
                give(slot, chunk, 64 if slot >= 4 else 32 + 8 * slot)

    for ch in range(8):
        @pl.when(there[ch])
        def _():
            halo_copy(rs, rr, bsem, brem, ch).start()

        @pl.when(jnp.logical_not(there[ch]))
        def _():
            rr[ch] = jnp.zeros((4, 32, 128), BF)

    for copy in first:
        copy.wait()
    for s in range(3):
        for n, (matrix, slot, count) in enumerate(RUNS[s]):
            kept = hh[pl.ds(matrix, count), sixteen(0, (cx, cy)[n]), :]
            got = [r1[n, d, pl.ds(slot, count)] for d in range(3)]
            s1[n, pl.ds(slot, count)] = kept + got[0] + got[1] + got[2]
    s1[0, pl.ds(14, 2)] = jnp.zeros((2, 16, 128), F32)
    s1[1, pl.ds(13, 3)] = jnp.zeros((3, 16, 128), F32)

    second = []
    for d in range(1, 4):
        for n in range(2):
            place = (cy, cx)[n]
            second.append(
                send(
                    s1.at[n, quarter((place + d) % 4)],
                    r2.at[n, d - 1],
                    17 + 2 * d - 1 + n,
                    (along_y, along_x)[n][d - 1],
                )
            )
    for copy in second:
        copy.start()

    for x in range(4):
        total = jnp.zeros((256, 256), F32)
        for kx in range(3):
            for ky in range(3):
                for w in range(2):
                    rows = pz[x + kx, pl.ds(ky, 4), pl.ds(w, 2)].reshape(256, 256)
                    total = total + nn(rows, wt[3 * kx + ky, w])
        co[x] = total.astype(BF).reshape(4, 2, 32, 256)
    for x in range(4):
        for hb in range(2):
            parts = [
                co[x, :, :, pl.ds(16 * hb, 16), pl.ds(128 * n, 128)].reshape(128, 128)
                for n in range(2)
            ]
            rows = nn(part_perm[...], jnp.concatenate(parts, axis=0)).reshape(16, 16, 128)
            block = iota((16, 16, 128), 0) + 16 * hb
            rows = rows * jnp.where(block < cnt[0], 1.0, 0.0)
            conv[pl.ds(16 * hb, 16), pl.ds(16 * x, 16), :] = rows.astype(BF)

    conv_copy = pltpu.make_async_copy(conv, conv_out, osem.at[0])
    conv_copy.start()

    for copy in second:
        copy.wait()
    for n in range(2):
        total = s1[n, quarter((cy, cx)[n])] + r2[n, 0] + r2[n, 1] + r2[n, 2]
        s2[n] = total.reshape(8, 8, 128)

    third = [
        send(s2.at[:, pl.ds((cz + d) % 8, 1)], r3.at[d - 1], 23 + d, along_z[d - 1])
        for d in range(1, 8)
    ]
    for copy in third:
        copy.start()

    for ch in range(8):
        @pl.when(there[ch])
        def _():
            halo_arrived(rs, rr, bsem, brem, ch).wait_recv()

    for ux in range(4):
        parts = []
        for uy in range(4):
            rows = de[pl.ds(ux * 16 + uy * 4, 4)].reshape(128, 128)
            for ch in range(8):
                wx, wy = WAYS[ch]
                if (wx != 0 and ux != side(wx)) or (wy != 0 and uy != side(wy)):
                    continue
                chunk = 0 if ch >= 4 else (uy if wx != 0 else ux)
                rows = rows + nn(bdt[ch], rr[ch, chunk])
            parts.append(rows.astype(BF).reshape(4, 32, 128))
        parts = jnp.concatenate(parts, axis=0)
        for hb in range(2):
            swapped = swap16(parts[:, 16 * hb : 16 * hb + 16])
            igrad[pl.ds(16 * hb, 16), pl.ds(16 * ux, 16), :] = swapped.astype(BF)

    igrad_copy = pltpu.make_async_copy(igrad, igrad_out, osem.at[1])
    igrad_copy.start()

    for copy in third:
        copy.wait()
    whole = s2[:, pl.ds(cz, 1)]
    for d in range(7):
        whole = whole + r3[d]
    tt[...] = (whole * (1.0 / math.sqrt(256 * 32 * 64))).reshape(16, 128).astype(BF)
    g3[pl.ds(cz, 1)] = tt[...][None]

    fourth = [send(tt, g3.at[cz], 30 + d, along_z[d - 1]) for d in range(1, 8)]
    for copy in fourth:
        copy.start()
    for copy in fourth:
        copy.wait()
    sums = g3[...].astype(F32)
    g2[0, quarter(cy)] = sums[:, :8].reshape(4, 16, 128).astype(BF)
    g2[1, quarter(cx)] = sums[:, 8:].reshape(4, 16, 128).astype(BF)

    def across(n, away):
        piece = g2.at[n, quarter(((cy, cx)[n] + 4 - away) % 4)]
        rows = sixteen(64 * core, (cx, cy)[n])
        copies = []
        for d in range(1, 4):
            copy = send(
                piece,
                kg.at[n, quarter(((cy, cx)[n] + 4 - away) % 4), rows, :],
                44 + 12 * n + 3 * away + d - 1,
                (along_x, along_y)[n][d - 1],
            )
            copy.start()
            copies.append(copy)
        return copies

    fifth = []
    for d in (1, 3, 2):
        for n in range(2):
            piece = g2.at[n, quarter((cy, cx)[n])]
            fifth.append(send(piece, piece, 36 + 2 * d + n, (along_y, along_x)[n][d - 1]))
    for copy in fifth:
        copy.start()
    sixth = [across(n, 0) for n in range(2)]
    for order, d in enumerate((1, 3, 2)):
        for n in range(2):
            fifth[2 * order + n].wait()
            sixth.append(across(n, d))

    last = []
    for n in range(2):
        rows = sixteen(64 * core, (cx, cy)[n])
        last.append(pltpu.make_async_copy(g2.at[n], kg.at[n, :, rows, :], osem.at[2 + n]))
        last.append(send(g2.at[n], kg.at[n, :, rows, :], 68 + n, sibling))
    for copy in last:
        copy.start()
    for d in (1, 3, 2):
        for n in range(2):
            for group in sixth[n::2]:
                group[d - 1].wait()
            rows = kg.at[n, :, sixteen(64 * core, ((cx, cy)[n] + 4 - d) % 4), :]
            forward = send(rows, rows, 68 + 2 * d + n, sibling)
            forward.start()
            last.append(forward)
    for copy in last + [conv_copy, igrad_copy]:
        copy.wait()

    for ch in range(8):
        @pl.when(there[ch])
        def _():
            halo_copy(hs, hr, hsem, hrem, ch).wait_send()
            halo_copy(rs, rr, bsem, brem, ch).wait_send()


def finish(conv, igrad, kg, conv_out, igrad_out, kgrad_out, conv_v, igrad_v, held, wide, sem):
    loads = []
    for s in range(3):
        slots = pl.ds(*((0, 5), (5, 5), (10, 4))[s])
        loads.append(pltpu.make_async_copy(kg.at[:, slots], held.at[:, slots], sem.at[s]))
    loads.append(pltpu.make_async_copy(conv, conv_v, sem.at[3]))
    loads.append(pltpu.make_async_copy(igrad, igrad_v, sem.at[4]))
    for copy in loads:
        copy.start()
    stores = []
    for s in range(3):
        loads[s].wait()
        for n, (matrix, slot, count) in enumerate(RUNS[s]):
            wide[pl.ds(matrix, count)] = held[n, pl.ds(slot, count)].astype(F32)
        part = pl.ds(9 * s, 9)
        stores.append(pltpu.make_async_copy(wide.at[part], kgrad_out.at[part], sem.at[5 + s]))
        stores[-1].start()
    for n, (src, dst) in enumerate(((conv_v, conv_out), (igrad_v, igrad_out))):
        loads[3 + n].wait()
        stores.append(pltpu.make_async_copy(src, dst, sem.at[8 + n]))
        stores[-1].start()
    for copy in stores:
        copy.wait()


def per_device(features, cotangent, kernel, block_count, neighbours, send_face, send_corner):
    vmem = pl.BlockSpec(memory_space=pltpu.VMEM)
    smem = pl.BlockSpec(memory_space=pltpu.SMEM)
    hbm = pl.BlockSpec(memory_space=pltpu.HBM)
    dma = pltpu.SemaphoreType.DMA
    blocks = (32, 64, 128)
    conv, igrad, kg = pl.pallas_call(
        body,
        out_shape=(
            jax.ShapeDtypeStruct(blocks, BF),
            jax.ShapeDtypeStruct(blocks, BF),
            jax.ShapeDtypeStruct((2, 16, 128, 128), BF),
        ),
        in_specs=[smem] * 3 + [hbm] * 4,
        out_specs=(hbm, hbm, hbm),
        scratch_shapes=[
            pltpu.VMEM(blocks, BF),
            pltpu.VMEM(blocks, BF),
            pltpu.VMEM((27, 128, 128), BF),
            pltpu.VMEM((32, 27), jnp.int32),
            pltpu.VMEM(blocks, BF),
            pltpu.VMEM(blocks, BF),
            pltpu.VMEM((64, 128, 128), BF),
            pltpu.VMEM((6, 6, 3, 32, 256), BF),
            pltpu.VMEM((4, 4, 2, 32, 256), BF),
            pltpu.VMEM((3, 256, 1024), BF),
            pltpu.VMEM((2, 256, 256), BF),
            pltpu.VMEM((9, 2, 256, 256), BF),
            pltpu.VMEM((27, 128, 128), F32),
            pltpu.VMEM((6, 6, 3, 32, 256), F32),
            pltpu.VMEM((64, 32, 128), F32),
            pltpu.VMEM((27, 32, 128), BF),
            pltpu.VMEM((27, 80, 256), BF),
            pltpu.VMEM((8, 32, 128), BF),
            pltpu.VMEM((8, 128, 32), BF),
            pltpu.VMEM((4, 4, 2, 32, 256), BF),
            pltpu.VMEM((256, 256), BF),
            pltpu.VMEM((256, 256), BF),
            pltpu.VMEM((256, 256), BF),
            pltpu.VMEM((8, 4, 32, 128), BF),
            pltpu.VMEM((8, 4, 32, 128), BF),
            pltpu.VMEM((8, 4, 32, 128), BF),
            pltpu.VMEM((8, 4, 32, 128), BF),
            pltpu.VMEM((27, 128, 128), F32),
            pltpu.VMEM((27, 64, 128), F32),
            pltpu.VMEM((27, 64, 128), F32),
            pltpu.VMEM((2, 3, 14, 16, 128), F32),
            pltpu.VMEM((2, 16, 16, 128), F32),
            pltpu.VMEM((2, 3, 4, 16, 128), F32),
            pltpu.VMEM((2, 8, 8, 128), F32),
            pltpu.VMEM((7, 2, 1, 8, 128), F32),
            pltpu.VMEM((16, 128), BF),
            pltpu.VMEM((8, 16, 128), BF),
            pltpu.VMEM((2, 16, 16, 128), BF),
            dma((4,)), dma((4,)), dma((8,)), dma((8,)), dma((8,)), dma((8,)),
            dma((3,)), dma((3,)), dma((76,)), dma((76,)),
        ],
        compiler_params=pltpu.CompilerParams(
            collective_id=0, has_side_effects=True, vmem_limit_bytes=62 * 1024 * 1024
        ),
        cost_estimate=pl.CostEstimate(
            flops=7_000_000_000, bytes_accessed=6_000_000, transcendentals=0
        ),
    )(
        block_count,
        send_face,
        jnp.swapaxes(send_corner, 1, 2),
        features.reshape(blocks),
        cotangent.reshape(blocks),
        kernel,
        neighbours,
    )
    conv, igrad, kgrad = pl.pallas_call(
        finish,
        out_shape=(
            jax.ShapeDtypeStruct(blocks, BF),
            jax.ShapeDtypeStruct(blocks, BF),
            jax.ShapeDtypeStruct((27, 128, 128), F32),
        ),
        in_specs=[hbm] * 3,
        out_specs=(hbm, hbm, hbm),
        scratch_shapes=[
            pltpu.VMEM(blocks, BF),
            pltpu.VMEM(blocks, BF),
            pltpu.VMEM((2, 16, 128, 128), BF),
            pltpu.VMEM((27, 128, 128), F32),
            dma((10,)),
        ],
        compiler_params=pltpu.CompilerParams(vmem_limit_bytes=62 * 1024 * 1024),
    )(conv, igrad, kg)
    return conv.reshape(2048, 128), igrad.reshape(2048, 128), kgrad


def solution(mesh):
    in_specs = (
        P(("gx", "gy"), None),
        P(("gx", "gy"), None),
        P(),
        P(("gx", "gy")),
        P(("gx", "gy"), None),
        P(("gx", "gy"), None, None),
        P(("gx", "gy"), None, None),
    )
    out_specs = (P(("gx", "gy"), None), P(("gx", "gy"), None), P())
    return jax.shard_map(
        per_device, mesh=mesh, in_specs=in_specs, out_specs=out_specs, check_vma=False
    )
```

time: 71.9 us -> 57.2 us (0.80)
  local copies, waits for them, and re-layouts: 7.49 us -> 0 us
  Pallas kernels: 61.9 us -> 55.5 us
  other arithmetic: 0.87 us -> 0 us
    unnamed x10 -> x0, local copies, waits for them, and re-layouts: 6.81 us -> none
    pallas_call x1 -> x2, Pallas kernels: 61.9 us -> 55.5 us  [the longest x1 52.9 us: per_device(): pl.pallas_call(body, out_shape=(jax.ShapeDtypeStruct(blocks, BF), jax.Sha...]
    concatenate x1 -> x0, other arithmetic: 0.79 us -> none  [per_device(): jnp.concatenate([neighbours, face, jnp.tile(corner, (4, 1))], axis=1)]
where the time goes in v1:
time: 57.2 us; the launch traced here: 57 us
  Pallas kernels  55.5 us (97%)
  between operations  1.45 us (3%)
    pallas_call x1, Pallas kernels, per_device(): pl.pallas_call(body, out_shape=(jax.ShapeDtypeStruct(blocks, BF), jax.Sha...  52.9 us
    pallas_call x1, Pallas kernels, per_device(): pl.pallas_call(finish, out_shape=(jax.ShapeDtypeStruct(blocks, BF), jax.S...  2.65 us

profile of v1, /device:TPU:1, one launch (start us, length us, event | category | flops | bytes accessed | tf_op | source)
XLA Modules:
  0.0 57.0 jit_solution(2902983921716172773)
XLA Ops:
  1.3 52.9 %shard_map.94 = (bf16[32,64,128]{2,1,0:T(8,128)(2,1)}, bf16[32,64,128]{2,1,0:T(8,128)(2,1)}, bf16[2,16,128,128]{3,2,1,0:T(8,128)(2,1)}) custom-call(s32[1]{0:T(128)S(6)} %copy.10.cnt, s32[1,4,8]{2,1,0:T(4,128)} %face.1, s32[1,2,4]{2,1,0:T(2,128)} %bitcast.9, bf16[32,64,128]{2,1,0:T(8,128)(2,1)} %bitcast.5, bf16[32,64,128]{2,1,0:T(8,128)(2,1)} %bitcast.6, ...), custom_call_target="tpu_custom_call" | custom-call | flops 7000000000 | bytes 6000000 | tf_op jit(solution)/shard_map/pallas_call | solution.py:626
  54.2 2.6 %shard_map.95 = (bf16[32,64,128]{2,1,0:T(8,128)(2,1)}, bf16[32,64,128]{2,1,0:T(8,128)(2,1)}, f32[27,128,128]{2,1,0:T(8,128)}) custom-call(bf16[32,64,128]{2,1,0:T(8,128)(2,1)} %get-tuple-element.9.conv, bf16[32,64,128]{2,1,0:T(8,128)(2,1)} %get-tuple-element.10.igrad, bf16[2,16,128,128]{3,2,1,0:T(8,128)(2,1)} %get-tuple-element.11.kg), custom_call_target="tpu_custom_call" | custom-call | tf_op jit(solution)/shard_map/pallas_call | solution.py:692

commit v2 on v1

--- a/solution.py
+++ b/solution.py
@@ -69,19 +69,43 @@
     return lax.broadcasted_iota(jnp.int32, shape, dim)
 
 
+def encode(rows):
+    largest = jnp.max(jnp.abs(rows.reshape(-1, 8, 128)), axis=0)
+    for step in (4, 2, 1):
+        largest = jnp.maximum(largest, pltpu.roll(largest, step, 0))
+    largest = jnp.maximum(largest, 1e-33)
+    scale = largest * (1.0 / 32000.0)
+    inverse = 32000.0 / largest
+    coded = jnp.round(rows.reshape(-1, 8, 128) * inverse[None]).reshape(-1, 128)
+    return coded.astype(jnp.int32).astype(jnp.int16), scale
+
+
+def decode(coded, scale):
+    rows = coded.astype(jnp.int32).astype(F32).reshape(-1, 8, 128)
+    return (rows * scale[None]).reshape(-1, 128)
+
+
 def body(
-    cnt, face, corner, feat_in, cot_in, ker_in, near_in,
+    cnt_in, face_in, corner_in, feat_in, cot_in, ker_in, near_in,
     conv_out, igrad_out, kg,
-    feat, cot, ker, near, conv, igrad,
+    cnt, face, corner, feat, cot, ker, near, conv, igrad,
     et, pz, gz, gt, gty, wt, di, dp, de, oh, oht, bd, bdt, co, perm, pair_perm, part_perm,
     hs, hr, rs, rr,
-    wd, rcore, hh, r1, s1, r2, s2, r3, tt, g3, g2,
+    wd, rcore, hh, q1, r1, s1, q2, r2, qs, rscale, s2, r3, tt, g3, g2,
     isem, osem, hsem, hrem, bsem, brem, csem, crem, asem, arem,
 ):
     loads = [
         pltpu.make_async_copy(src, dst, isem.at[n])
         for n, (src, dst) in enumerate(
-            ((feat_in, feat), (cot_in, cot), (near_in, near), (ker_in, ker))
+            (
+                (feat_in, feat),
+                (cot_in, cot),
+                (near_in, near),
+                (ker_in, ker),
+                (face_in, face),
+                (corner_in, corner),
+                (cnt_in, cnt),
+            )
         )
     ]
     for copy in loads:
@@ -123,6 +147,8 @@
 
     r32, c32 = iota((32, 128), 0), iota((32, 128), 1)
     same_z = (r32 >> 3) == (c32 >> 5)
+    loads[4].wait()
+    loads[5].wait()
     for ch in range(8):
         index = jnp.full((32, 128), -1, jnp.int32)
         for n in range(8 if ch < 4 else 2):
@@ -183,6 +209,7 @@
         def _():
             halo_copy(hs, hr, hsem, hrem, ch).start()
 
+    loads[6].wait()
     lives = [jnp.where(iota((16, 128), 0) + 16 * hb < cnt[0], 1.0, 0.0) for hb in range(2)]
     loads[1].wait()
     for x in range(4):
@@ -258,7 +285,7 @@
             ]
             for n, value in enumerate(blocks_of(*sums)):
                 if kx == 1 and ky == 1:
-                    wd[9 * kx + 3 * ky + n] = value.T
+                    wd[9 * kx + 3 * ky + n] = value
                 else:
                     di[9 * kx + 3 * ky + n] = value
 
@@ -315,22 +342,11 @@
     def quarter(index):
         return pl.ds(4 * index, 4)
 
-    first = []
-
     def core_sum(s):
         core_copy(s).wait()
-        hh[pl.ds(9 * s, 9)] = wd[pl.ds(9 * s, 9), pl.ds(mine, 64), :] + rcore[pl.ds(9 * s, 9)]
         for n, (matrix, slot, count) in enumerate(RUNS[s]):
-            for d in range(1, 4):
-                place = (cx, cy)[n]
-                copy = send(
-                    hh.at[pl.ds(matrix, count), sixteen(0, (place + d) % 4), :],
-                    r1.at[n, d - 1, pl.ds(slot, count)],
-                    6 * s + 3 * n + d - 1,
-                    (along_x, along_y)[n][d - 1],
-                )
-                copy.start()
-                first.append(copy)
+            kept = wd[pl.ds(matrix, count), pl.ds(mine, 64), :]
+            hh[n, pl.ds(slot, count)] = kept + rcore[pl.ds(matrix, count)]
 
     def outer_sums(kx, ky, w):
         total = None
@@ -351,10 +367,32 @@
             value = blocks_of(outer_sums(s, ky, 0), outer_sums(s, ky, 1))
             for n in range(3):
                 j = 9 * s + 3 * ky + n
-                wd[j] = (di[j] + value[n]).T
+                wd[j] = di[j] + value[n]
         core_copy(s).start()
     for s in (1, 0, 2):
         core_sum(s)
+
+    far_first = (2, 1, 3)
+    first = []
+    for n in range(2):
+        size = (14, 13)[n]
+        for d in far_first:
+            rows = sixteen(0, ((cx, cy)[n] + d) % 4)
+            coded, scale = encode(hh[n, pl.ds(0, size), rows, :].reshape(-1, 128))
+            q1[n, d - 1, pl.ds(0, size)] = coded.reshape(size, 16, 128)
+            qs[0, n, d - 1] = scale
+            device = (along_x, along_y)[n][d - 1]
+            first.append(
+                send(
+                    q1.at[n, d - 1, pl.ds(0, size)],
+                    r1.at[n, d - 1, pl.ds(0, size)],
+                    3 * n + d - 1,
+                    device,
+                )
+            )
+            first.append(send(qs.at[0, n, d - 1], rscale.at[0, n, d - 1], 6 + 3 * n + d - 1, device))
+            first[-2].start()
+            first[-1].start()
 
     def weights(j, carry):
         low, mid, high = ker[3 * j], ker[3 * j + 1], ker[3 * j + 2]
@@ -440,28 +478,26 @@
 
     for copy in first:
         copy.wait()
-    for s in range(3):
-        for n, (matrix, slot, count) in enumerate(RUNS[s]):
-            kept = hh[pl.ds(matrix, count), sixteen(0, (cx, cy)[n]), :]
-            got = [r1[n, d, pl.ds(slot, count)] for d in range(3)]
-            s1[n, pl.ds(slot, count)] = kept + got[0] + got[1] + got[2]
-    s1[0, pl.ds(14, 2)] = jnp.zeros((2, 16, 128), F32)
-    s1[1, pl.ds(13, 3)] = jnp.zeros((3, 16, 128), F32)
+    for n in range(2):
+        size = (14, 13)[n]
+        total = hh[n, pl.ds(0, size), sixteen(0, (cx, cy)[n]), :]
+        for d in range(3):
+            got = decode(r1[n, d, pl.ds(0, size)].reshape(-1, 128), rscale[0, n, d])
+            total = total + got.reshape(size, 16, 128)
+        s1[n, pl.ds(0, size)] = total
+        s1[n, pl.ds(size, 16 - size)] = jnp.zeros((16 - size, 16, 128), F32)
 
     second = []
-    for d in range(1, 4):
-        for n in range(2):
-            place = (cy, cx)[n]
-            second.append(
-                send(
-                    s1.at[n, quarter((place + d) % 4)],
-                    r2.at[n, d - 1],
-                    17 + 2 * d - 1 + n,
-                    (along_y, along_x)[n][d - 1],
-                )
-            )
-    for copy in second:
-        copy.start()
+    for n in range(2):
+        for d in far_first:
+            coded, scale = encode(s1[n, quarter(((cy, cx)[n] + d) % 4)].reshape(64, 128))
+            q2[n, d - 1] = coded.reshape(4, 16, 128)
+            qs[1, n, d - 1] = scale
+            device = (along_y, along_x)[n][d - 1]
+            second.append(send(q2.at[n, d - 1], r2.at[n, d - 1], 12 + 3 * n + d - 1, device))
+            second.append(send(qs.at[1, n, d - 1], rscale.at[1, n, d - 1], 18 + 3 * n + d - 1, device))
+            second[-2].start()
+            second[-1].start()
 
     for x in range(4):
         total = jnp.zeros((256, 256), F32)
@@ -488,12 +524,14 @@
     for copy in second:
         copy.wait()
     for n in range(2):
-        total = s1[n, quarter((cy, cx)[n])] + r2[n, 0] + r2[n, 1] + r2[n, 2]
+        total = s1[n, quarter((cy, cx)[n])].reshape(64, 128)
+        for d in range(3):
+            total = total + decode(r2[n, d].reshape(64, 128), rscale[1, n, d])
         s2[n] = total.reshape(8, 8, 128)
 
     third = [
         send(s2.at[:, pl.ds((cz + d) % 8, 1)], r3.at[d - 1], 23 + d, along_z[d - 1])
-        for d in range(1, 8)
+        for d in (4, 3, 5, 2, 6, 1, 7)
     ]
     for copy in third:
         copy.start()
@@ -530,7 +568,9 @@
     tt[...] = (whole * (1.0 / math.sqrt(256 * 32 * 64))).reshape(16, 128).astype(BF)
     g3[pl.ds(cz, 1)] = tt[...][None]
 
-    fourth = [send(tt, g3.at[cz], 30 + d, along_z[d - 1]) for d in range(1, 8)]
+    fourth = [
+        send(tt, g3.at[cz], 30 + d, along_z[d - 1]) for d in (4, 3, 5, 2, 6, 1, 7)
+    ]
     for copy in fourth:
         copy.start()
     for copy in fourth:
@@ -542,8 +582,8 @@
     def across(n, away):
         piece = g2.at[n, quarter(((cy, cx)[n] + 4 - away) % 4)]
         rows = sixteen(64 * core, (cx, cy)[n])
-        copies = []
-        for d in range(1, 4):
+        copies = {}
+        for d in far_first:
             copy = send(
                 piece,
                 kg.at[n, quarter(((cy, cx)[n] + 4 - away) % 4), rows, :],
@@ -551,20 +591,19 @@
                 (along_x, along_y)[n][d - 1],
             )
             copy.start()
-            copies.append(copy)
+            copies[d] = copy
         return copies
 
-    fifth = []
+    fifth = {}
+    for d in far_first:
+        for n in range(2):
+            piece = g2.at[n, quarter((cy, cx)[n])]
+            fifth[d, n] = send(piece, piece, 36 + 2 * d + n, (along_y, along_x)[n][d - 1])
+            fifth[d, n].start()
+    sixth = [across(n, 0) for n in range(2)]
     for d in (1, 3, 2):
         for n in range(2):
-            piece = g2.at[n, quarter((cy, cx)[n])]
-            fifth.append(send(piece, piece, 36 + 2 * d + n, (along_y, along_x)[n][d - 1]))
-    for copy in fifth:
-        copy.start()
-    sixth = [across(n, 0) for n in range(2)]
-    for order, d in enumerate((1, 3, 2)):
-        for n in range(2):
-            fifth[2 * order + n].wait()
+            fifth[d, n].wait()
             sixth.append(across(n, d))
 
     last = []
@@ -577,7 +616,7 @@
     for d in (1, 3, 2):
         for n in range(2):
             for group in sixth[n::2]:
-                group[d - 1].wait()
+                group[d].wait()
             rows = kg.at[n, :, sixteen(64 * core, ((cx, cy)[n] + 4 - d) % 4), :]
             forward = send(rows, rows, 68 + 2 * d + n, sibling)
             forward.start()
@@ -605,7 +644,8 @@
     for s in range(3):
         loads[s].wait()
         for n, (matrix, slot, count) in enumerate(RUNS[s]):
-            wide[pl.ds(matrix, count)] = held[n, pl.ds(slot, count)].astype(F32)
+            for m in range(count):
+                wide[matrix + m] = held[n, slot + m].astype(F32).T
         part = pl.ds(9 * s, 9)
         stores.append(pltpu.make_async_copy(wide.at[part], kgrad_out.at[part], sem.at[5 + s]))
         stores[-1].start()
@@ -619,7 +659,6 @@
 
 def per_device(features, cotangent, kernel, block_count, neighbours, send_face, send_corner):
     vmem = pl.BlockSpec(memory_space=pltpu.VMEM)
-    smem = pl.BlockSpec(memory_space=pltpu.SMEM)
     hbm = pl.BlockSpec(memory_space=pltpu.HBM)
     dma = pltpu.SemaphoreType.DMA
     blocks = (32, 64, 128)
@@ -630,9 +669,12 @@
             jax.ShapeDtypeStruct(blocks, BF),
             jax.ShapeDtypeStruct((2, 16, 128, 128), BF),
         ),
-        in_specs=[smem] * 3 + [hbm] * 4,
-        out_specs=(hbm, hbm, hbm),
+        in_specs=[hbm] * 7,
+        out_specs=(hbm,) * 3,
         scratch_shapes=[
+            pltpu.SMEM((1,), jnp.int32),
+            pltpu.SMEM((1, 4, 8), jnp.int32),
+            pltpu.SMEM((1, 2, 4), jnp.int32),
             pltpu.VMEM(blocks, BF),
             pltpu.VMEM(blocks, BF),
             pltpu.VMEM((27, 128, 128), BF),
@@ -662,16 +704,20 @@
             pltpu.VMEM((8, 4, 32, 128), BF),
             pltpu.VMEM((27, 128, 128), F32),
             pltpu.VMEM((27, 64, 128), F32),
-            pltpu.VMEM((27, 64, 128), F32),
-            pltpu.VMEM((2, 3, 14, 16, 128), F32),
+            pltpu.VMEM((2, 14, 64, 128), F32),
+            pltpu.VMEM((2, 3, 14, 16, 128), jnp.int16),
+            pltpu.VMEM((2, 3, 14, 16, 128), jnp.int16),
             pltpu.VMEM((2, 16, 16, 128), F32),
-            pltpu.VMEM((2, 3, 4, 16, 128), F32),
+            pltpu.VMEM((2, 3, 4, 16, 128), jnp.int16),
+            pltpu.VMEM((2, 3, 4, 16, 128), jnp.int16),
+            pltpu.VMEM((2, 2, 3, 8, 128), F32),
+            pltpu.VMEM((2, 2, 3, 8, 128), F32),
             pltpu.VMEM((2, 8, 8, 128), F32),
             pltpu.VMEM((7, 2, 1, 8, 128), F32),
             pltpu.VMEM((16, 128), BF),
             pltpu.VMEM((8, 16, 128), BF),
             pltpu.VMEM((2, 16, 16, 128), BF),
-            dma((4,)), dma((4,)), dma((8,)), dma((8,)), dma((8,)), dma((8,)),
+            dma((7,)), dma((4,)), dma((8,)), dma((8,)), dma((8,)), dma((8,)),
             dma((3,)), dma((3,)), dma((76,)), dma((76,)),
         ],
         compiler_params=pltpu.CompilerParams(

time: 57.2 us -> 54.2 us (0.948)
  Pallas kernels: 55.5 us -> 52.6 us
    pallas_call x1, Pallas kernels: 52.9 us -> 49.8 us  [per_device(): pl.pallas_call(body, out_shape=(jax.ShapeDtypeStruct(blocks, BF), jax.Sha...]
where the time goes in v2:
time: 54.2 us; the launch traced here: 54.1 us
  Pallas kernels  52.6 us (97%)
  between operations  1.45 us (3%)
    pallas_call x1, Pallas kernels, per_device(): pl.pallas_call(body, out_shape=(jax.ShapeDtypeStruct(blocks, BF), jax.Sha...  49.8 us
    pallas_call x1, Pallas kernels, per_device(): pl.pallas_call(finish, out_shape=(jax.ShapeDtypeStruct(blocks, BF), jax.S...  2.78 us

profile of v2, /device:TPU:1, one launch (start us, length us, event | category | flops | bytes accessed | tf_op | source)
XLA Modules:
  0.0 54.1 jit_solution(2474377522097615162)
XLA Ops:
  1.3 49.8 %shard_map.94 = (bf16[32,64,128]{2,1,0:T(8,128)(2,1)}, bf16[32,64,128]{2,1,0:T(8,128)(2,1)}, bf16[2,16,128,128]{3,2,1,0:T(8,128)(2,1)}) custom-call(s32[1]{0:T(128)S(6)} %copy.10.cnt_in, s32[1,4,8]{2,1,0:T(4,128)} %face_in.1, s32[1,2,4]{2,1,0:T(2,128)} %bitcast.9, bf16[32,64,128]{2,1,0:T(8,128)(2,1)} %bitcast.5, bf16[32,64,128]{2,1,0:T(8,128)(2,1)} %bitcast.6, ...), custom_call_target="tpu_custom_call" | custom-call | flops 7000000000 | bytes 6000000 | tf_op jit(solution)/shard_map/pallas_call | solution.py:665
  51.1 2.8 %shard_map.95 = (bf16[32,64,128]{2,1,0:T(8,128)(2,1)}, bf16[32,64,128]{2,1,0:T(8,128)(2,1)}, f32[27,128,128]{2,1,0:T(8,128)}) custom-call(bf16[32,64,128]{2,1,0:T(8,128)(2,1)} %get-tuple-element.9.conv, bf16[32,64,128]{2,1,0:T(8,128)(2,1)} %get-tuple-element.10.igrad, bf16[2,16,128,128]{3,2,1,0:T(8,128)(2,1)} %get-tuple-element.11.kg), custom_call_target="tpu_custom_call" | custom-call | tf_op jit(solution)/shard_map/pallas_call | solution.py:738

commit v3 on v2

--- a/solution.py
+++ b/solution.py
@@ -86,25 +86,24 @@
 
 
 def body(
-    cnt_in, face_in, corner_in, feat_in, cot_in, ker_in, near_in,
+    face_in, corner_in, feat_in, cot_in, ker_in, near_in,
     conv_out, igrad_out, kg,
-    cnt, face, corner, feat, cot, ker, near, conv, igrad,
+    face, corner, feat, cot, ker, near, live, conv, igrad,
     et, pz, gz, gt, gty, wt, di, dp, de, oh, oht, bd, bdt, co, perm, pair_perm, part_perm,
     hs, hr, rs, rr,
-    wd, rcore, hh, q1, r1, s1, q2, r2, qs, rscale, s2, r3, tt, g3, g2,
+    wd, rcore, hh, q1, r1, s1, q2, r2, qs, rscale, s2, q3, qs3, r3, rscale3, g2,
     isem, osem, hsem, hrem, bsem, brem, csem, crem, asem, arem,
 ):
     loads = [
         pltpu.make_async_copy(src, dst, isem.at[n])
         for n, (src, dst) in enumerate(
             (
-                (feat_in, feat),
-                (cot_in, cot),
-                (near_in, near),
-                (ker_in, ker),
                 (face_in, face),
                 (corner_in, corner),
-                (cnt_in, cnt),
+                (feat_in, feat),
+                (near_in, near),
+                (cot_in, cot),
+                (ker_in, ker),
             )
         )
     ]
@@ -130,7 +129,7 @@
     ]
 
     barrier = pltpu.get_barrier_semaphore()
-    greet = [sibling] + along_x + along_y + along_z
+    greet = [along_z[n] for n in (3, 2, 4, 1, 5, 0, 6)] + along_x + along_y + [sibling]
     greet += [((gx + wx + 64) % 64, (gy + wy + 4) % 4) for wx, wy in WAYS]
     for other in greet:
         pl.semaphore_signal(barrier, inc=1, device_id=other, device_id_type=MESH)
@@ -145,10 +144,16 @@
     def swap16(v):
         return nn(perm[...], v.reshape(256, 128)).reshape(16, 16, 128)
 
+    def clear(u, carry):
+        et[u, pl.ds(32, 96), :] = jnp.zeros((96, 128), BF)
+        return carry
+
+    lax.fori_loop(0, 64, clear, 0)
+
     r32, c32 = iota((32, 128), 0), iota((32, 128), 1)
     same_z = (r32 >> 3) == (c32 >> 5)
-    loads[4].wait()
-    loads[5].wait()
+    loads[0].wait()
+    loads[1].wait()
     for ch in range(8):
         index = jnp.full((32, 128), -1, jnp.int32)
         for n in range(8 if ch < 4 else 2):
@@ -159,7 +164,7 @@
         bd[ch] = pick
         bdt[ch] = nt(eye, pick).astype(BF)
 
-    loads[0].wait()
+    loads[2].wait()
     for hb in range(2):
         for ug in range(4):
             rows = swap16(feat[pl.ds(16 * hb, 16), pl.ds(16 * ug, 16), :])
@@ -209,24 +214,26 @@
         def _():
             halo_copy(hs, hr, hsem, hrem, ch).start()
 
-    loads[6].wait()
-    lives = [jnp.where(iota((16, 128), 0) + 16 * hb < cnt[0], 1.0, 0.0) for hb in range(2)]
-    loads[1].wait()
+    loads[3].wait()
+    live[...] = jnp.where(near[:, 13:14] == r32, 1.0, 0.0)
+    lives = [live[pl.ds(16 * hb, 16), :] for hb in range(2)]
+    loads[4].wait()
     for x in range(4):
         for hb in range(2):
             rows = cot[pl.ds(16 * hb, 16), pl.ds(16 * x, 16), :].reshape(256, 128)
             rows = nn(pair_perm[...], rows).reshape(2, 4, 2, 16, 128) * lives[hb]
             for n in range(2):
                 gz[x, :, :, pl.ds(16 * hb, 16), pl.ds(128 * n, 128)] = rows[n].astype(BF)
+    for x in range(4):
         turned = nt(eye256, gz[x].reshape(256, 256))
         place = pl.ds(256 * x, 256)
-        gt[0, :, place] = jnp.where(c256 < 64, 0.0, turned).astype(BF)
-        gt[1, :, place] = turned.astype(BF)
-        gt[2, :, place] = jnp.where(c256 < 192, turned, 0.0).astype(BF)
+        gt[:, place] = turned.astype(BF)
     for n, y in enumerate((0, 3)):
-        gty[n] = nt(eye256, gz[:, y].reshape(256, 256)).astype(BF)
-
-    loads[2].wait()
+        turned = nt(eye256, gz[:, y].reshape(256, 256))
+        gty[n, 0] = jnp.where(c256 < 64, 0.0, turned).astype(BF)
+        gty[n, 1] = turned.astype(BF)
+        gty[n, 2] = jnp.where(c256 < 192, turned, 0.0).astype(BF)
+
     columns = c32 + jnp.where(c32 >= 32, 1, 0)
     for o in range(27):
         oh[o] = onehot(near[:, o : o + 1] == columns)
@@ -239,12 +246,6 @@
         if len(offsets) == 1:
             return oh[offsets[0]]
         return jnp.concatenate([oh[o] for o in offsets], axis=0)
-
-    def clear(u, carry):
-        et[u, pl.ds(32, 96), :] = jnp.zeros((96, 128), BF)
-        return carry
-
-    lax.fori_loop(0, 64, clear, 0)
 
     def inner(found):
         return [r for r in found if 1 <= r[0] <= 4 and 1 <= r[1] <= 4]
@@ -265,6 +266,19 @@
                 picks = stacked([r[3] for r in found])[:, :32]
                 keep(nn(picks, et[ux * 16 + uy * 4 + uz, pl.ds(0, 32)]).astype(BF), found)
 
+    mine = pl.multiple_of(64 * core, 64)
+    other = pl.multiple_of(64 - 64 * core, 64)
+
+    def core_copy(s):
+        return pltpu.make_async_remote_copy(
+            src_ref=wd.at[pl.ds(9 * s, 9), pl.ds(other, 64), :],
+            dst_ref=rcore.at[pl.ds(9 * s, 9)],
+            send_sem=csem.at[s],
+            recv_sem=crem.at[s],
+            device_id=sibling,
+            device_id_type=MESH,
+        )
+
     def blocks_of(d0, d1):
         return (
             d0[:128, :128] + d0[128:, 128:],
@@ -275,7 +289,7 @@
     for kx in range(3):
         x0, x1 = ((1, 4), (0, 4), (0, 3))[kx]
         for ky in range(3):
-            left = gt[ky, :, pl.ds(256 * x0, 256 * (x1 - x0))]
+            left = gt[:, pl.ds(256 * x0, 256 * (x1 - x0))]
             sums = [
                 nn(
                     left,
@@ -313,19 +327,6 @@
                     picks = stacked([r[3] for r in found])
                     keep(nn(picks, et[ux * 16 + uy * 4 + uz]).astype(BF), found)
 
-    mine = pl.multiple_of(64 * core, 64)
-    other = pl.multiple_of(64 - 64 * core, 64)
-
-    def core_copy(s):
-        return pltpu.make_async_remote_copy(
-            src_ref=wd.at[pl.ds(9 * s, 9), pl.ds(other, 64), :],
-            dst_ref=rcore.at[pl.ds(9 * s, 9)],
-            send_sem=csem.at[s],
-            recv_sem=crem.at[s],
-            device_id=sibling,
-            device_id_type=MESH,
-        )
-
     def send(src, dst, n, device):
         return pltpu.make_async_remote_copy(
             src_ref=src,
@@ -352,11 +353,11 @@
         total = None
         if ky != 1:
             rows = pz[pl.ds(kx, 4), (0, None, 5)[ky], pl.ds(w, 2)].reshape(256, 256)
-            total = nn(gty[ky // 2], rows)
+            total = nn(gty[ky // 2, kx], rows)
         if kx != 1:
             x, px = ((0, 0), None, (3, 5))[kx]
             rows = pz[px, pl.ds(ky, 4), pl.ds(w, 2)].reshape(256, 256)
-            term = nn(gt[ky, :, pl.ds(256 * x, 256)], rows)
+            term = nn(gt[:, pl.ds(256 * x, 256)], rows)
             total = term if total is None else total + term
         return total
 
@@ -407,7 +408,7 @@
         wt[j, 1, pl.ds(128, 128), pl.ds(128, 128)] = high
         return carry
 
-    loads[3].wait()
+    loads[5].wait()
     lax.fori_loop(0, 9, weights, 0)
 
     for tx in range(3):
@@ -432,6 +433,29 @@
                         one = nt(gz[px - kx].reshape(256, 256), wt[3 * kx + ky, w])
                         term = one if term is None else term + one
                 dp[px, pl.ds(ky, 4), pl.ds(w, 2)] += term.reshape(4, 2, 32, 256)
+
+    for copy in first:
+        copy.wait()
+    for n in range(2):
+        size = (14, 13)[n]
+        total = hh[n, pl.ds(0, size), sixteen(0, (cx, cy)[n]), :]
+        for d in range(3):
+            got = decode(r1[n, d, pl.ds(0, size)].reshape(-1, 128), rscale[0, n, d])
+            total = total + got.reshape(size, 16, 128)
+        s1[n, pl.ds(0, size)] = total
+        s1[n, pl.ds(size, 16 - size)] = jnp.zeros((16 - size, 16, 128), F32)
+
+    second = []
+    for n in range(2):
+        for d in far_first:
+            coded, scale = encode(s1[n, quarter(((cy, cx)[n] + d) % 4)].reshape(64, 128))
+            q2[n, d - 1] = coded.reshape(4, 16, 128)
+            qs[1, n, d - 1] = scale
+            device = (along_y, along_x)[n][d - 1]
+            second.append(send(q2.at[n, d - 1], r2.at[n, d - 1], 12 + 3 * n + d - 1, device))
+            second.append(send(qs.at[1, n, d - 1], rscale.at[1, n, d - 1], 18 + 3 * n + d - 1, device))
+            second[-2].start()
+            second[-1].start()
 
     for ux in range(4):
         for uy in range(4):
@@ -476,37 +500,40 @@
         def _():
             rr[ch] = jnp.zeros((4, 32, 128), BF)
 
-    for copy in first:
-        copy.wait()
-    for n in range(2):
-        size = (14, 13)[n]
-        total = hh[n, pl.ds(0, size), sixteen(0, (cx, cy)[n]), :]
-        for d in range(3):
-            got = decode(r1[n, d, pl.ds(0, size)].reshape(-1, 128), rscale[0, n, d])
-            total = total + got.reshape(size, 16, 128)
-        s1[n, pl.ds(0, size)] = total
-        s1[n, pl.ds(size, 16 - size)] = jnp.zeros((16 - size, 16, 128), F32)
-
-    second = []
-    for n in range(2):
-        for d in far_first:
-            coded, scale = encode(s1[n, quarter(((cy, cx)[n] + d) % 4)].reshape(64, 128))
-            q2[n, d - 1] = coded.reshape(4, 16, 128)
-            qs[1, n, d - 1] = scale
-            device = (along_y, along_x)[n][d - 1]
-            second.append(send(q2.at[n, d - 1], r2.at[n, d - 1], 12 + 3 * n + d - 1, device))
-            second.append(send(qs.at[1, n, d - 1], rscale.at[1, n, d - 1], 18 + 3 * n + d - 1, device))
-            second[-2].start()
-            second[-1].start()
-
-    for x in range(4):
+    def convolve(x):
         total = jnp.zeros((256, 256), F32)
         for kx in range(3):
             for ky in range(3):
                 for w in range(2):
                     rows = pz[x + kx, pl.ds(ky, 4), pl.ds(w, 2)].reshape(256, 256)
                     total = total + nn(rows, wt[3 * kx + ky, w])
-        co[x] = total.astype(BF).reshape(4, 2, 32, 256)
+        alive = jnp.concatenate([live[...], live[...]], axis=1)
+        co[x] = (total.reshape(4, 2, 32, 256) * alive).astype(BF)
+    convolve(0)
+    convolve(1)
+
+    for copy in second:
+        copy.wait()
+    for n in range(2):
+        total = s1[n, quarter((cy, cx)[n])].reshape(64, 128)
+        for d in range(3):
+            total = total + decode(r2[n, d].reshape(64, 128), rscale[1, n, d])
+        s2[n] = total
+
+    coded, scale = encode(s2[...].reshape(128, 128))
+    q3[...] = coded
+    qs3[...] = scale
+    r3[pl.ds(cz, 1)] = coded[None]
+    rscale3[pl.ds(cz, 1)] = scale[None]
+    third = []
+    for d in (4, 3, 5, 2, 6, 1, 7):
+        third.append(send(q3, r3.at[cz], 23 + d, along_z[d - 1]))
+        third.append(send(qs3, rscale3.at[cz], 30 + d, along_z[d - 1]))
+    for copy in third:
+        copy.start()
+
+    convolve(2)
+    convolve(3)
     for x in range(4):
         for hb in range(2):
             parts = [
@@ -514,27 +541,10 @@
                 for n in range(2)
             ]
             rows = nn(part_perm[...], jnp.concatenate(parts, axis=0)).reshape(16, 16, 128)
-            block = iota((16, 16, 128), 0) + 16 * hb
-            rows = rows * jnp.where(block < cnt[0], 1.0, 0.0)
             conv[pl.ds(16 * hb, 16), pl.ds(16 * x, 16), :] = rows.astype(BF)
 
     conv_copy = pltpu.make_async_copy(conv, conv_out, osem.at[0])
     conv_copy.start()
-
-    for copy in second:
-        copy.wait()
-    for n in range(2):
-        total = s1[n, quarter((cy, cx)[n])].reshape(64, 128)
-        for d in range(3):
-            total = total + decode(r2[n, d].reshape(64, 128), rscale[1, n, d])
-        s2[n] = total.reshape(8, 8, 128)
-
-    third = [
-        send(s2.at[:, pl.ds((cz + d) % 8, 1)], r3.at[d - 1], 23 + d, along_z[d - 1])
-        for d in (4, 3, 5, 2, 6, 1, 7)
-    ]
-    for copy in third:
-        copy.start()
 
     for ch in range(8):
         @pl.when(there[ch])
@@ -562,22 +572,12 @@
 
     for copy in third:
         copy.wait()
-    whole = s2[:, pl.ds(cz, 1)]
-    for d in range(7):
-        whole = whole + r3[d]
-    tt[...] = (whole * (1.0 / math.sqrt(256 * 32 * 64))).reshape(16, 128).astype(BF)
-    g3[pl.ds(cz, 1)] = tt[...][None]
-
-    fourth = [
-        send(tt, g3.at[cz], 30 + d, along_z[d - 1]) for d in (4, 3, 5, 2, 6, 1, 7)
-    ]
-    for copy in fourth:
-        copy.start()
-    for copy in fourth:
-        copy.wait()
-    sums = g3[...].astype(F32)
-    g2[0, quarter(cy)] = sums[:, :8].reshape(4, 16, 128).astype(BF)
-    g2[1, quarter(cx)] = sums[:, 8:].reshape(4, 16, 128).astype(BF)
+    whole = decode(r3[0], rscale3[0])
+    for z in range(1, 8):
+        whole = whole + decode(r3[z], rscale3[z])
+    whole = (whole * (1.0 / math.sqrt(256 * 32 * 64))).reshape(2, 4, 16, 128).astype(BF)
+    g2[0, quarter(cy)] = whole[0]
+    g2[1, quarter(cx)] = whole[1]
 
     def across(n, away):
         piece = g2.at[n, quarter(((cy, cx)[n] + 4 - away) % 4)]
@@ -632,27 +632,32 @@
 
 
 def finish(conv, igrad, kg, conv_out, igrad_out, kgrad_out, conv_v, igrad_v, held, wide, sem):
-    loads = []
+    places = [(conv, conv_v), (igrad, igrad_v)]
     for s in range(3):
         slots = pl.ds(*((0, 5), (5, 5), (10, 4))[s])
-        loads.append(pltpu.make_async_copy(kg.at[:, slots], held.at[:, slots], sem.at[s]))
-    loads.append(pltpu.make_async_copy(conv, conv_v, sem.at[3]))
-    loads.append(pltpu.make_async_copy(igrad, igrad_v, sem.at[4]))
-    for copy in loads:
-        copy.start()
+        places.append((kg.at[:, slots], held.at[:, slots]))
+    loads = [pltpu.make_async_copy(*places[n], sem.at[n]) for n in range(5)]
+    for n in (2, 0, 1, 3, 4):
+        loads[n].start()
+    eye = onehot(iota((128, 128), 0) == iota((128, 128), 1))
     stores = []
+
+    def store(src, dst):
+        stores.append(pltpu.make_async_copy(src, dst, sem.at[5 + len(stores)]))
+        stores[-1].start()
+
     for s in range(3):
-        loads[s].wait()
+        loads[2 + s].wait()
         for n, (matrix, slot, count) in enumerate(RUNS[s]):
             for m in range(count):
-                wide[matrix + m] = held[n, slot + m].astype(F32).T
+                wide[matrix + m] = nt(eye, held[n, slot + m])
         part = pl.ds(9 * s, 9)
-        stores.append(pltpu.make_async_copy(wide.at[part], kgrad_out.at[part], sem.at[5 + s]))
-        stores[-1].start()
-    for n, (src, dst) in enumerate(((conv_v, conv_out), (igrad_v, igrad_out))):
-        loads[3 + n].wait()
-        stores.append(pltpu.make_async_copy(src, dst, sem.at[8 + n]))
-        stores[-1].start()
+        store(wide.at[part], kgrad_out.at[part])
+        if s == 0:
+            loads[0].wait()
+            store(conv_v, conv_out)
+            loads[1].wait()
+            store(igrad_v, igrad_out)
     for copy in stores:
         copy.wait()
 
@@ -669,23 +674,23 @@
             jax.ShapeDtypeStruct(blocks, BF),
             jax.ShapeDtypeStruct((2, 16, 128, 128), BF),
         ),
-        in_specs=[hbm] * 7,
+        in_specs=[hbm] * 6,
         out_specs=(hbm,) * 3,
         scratch_shapes=[
-            pltpu.SMEM((1,), jnp.int32),
             pltpu.SMEM((1, 4, 8), jnp.int32),
             pltpu.SMEM((1, 2, 4), jnp.int32),
             pltpu.VMEM(blocks, BF),
             pltpu.VMEM(blocks, BF),
             pltpu.VMEM((27, 128, 128), BF),
             pltpu.VMEM((32, 27), jnp.int32),
+            pltpu.VMEM((32, 128), F32),
             pltpu.VMEM(blocks, BF),
             pltpu.VMEM(blocks, BF),
             pltpu.VMEM((64, 128, 128), BF),
             pltpu.VMEM((6, 6, 3, 32, 256), BF),
             pltpu.VMEM((4, 4, 2, 32, 256), BF),
-            pltpu.VMEM((3, 256, 1024), BF),
-            pltpu.VMEM((2, 256, 256), BF),
+            pltpu.VMEM((256, 1024), BF),
+            pltpu.VMEM((2, 3, 256, 256), BF),
             pltpu.VMEM((9, 2, 256, 256), BF),
             pltpu.VMEM((27, 128, 128), F32),
             pltpu.VMEM((6, 6, 3, 32, 256), F32),
@@ -712,10 +717,11 @@
             pltpu.VMEM((2, 3, 4, 16, 128), jnp.int16),
             pltpu.VMEM((2, 2, 3, 8, 128), F32),
             pltpu.VMEM((2, 2, 3, 8, 128), F32),
-            pltpu.VMEM((2, 8, 8, 128), F32),
-            pltpu.VMEM((7, 2, 1, 8, 128), F32),
-            pltpu.VMEM((16, 128), BF),
-            pltpu.VMEM((8, 16, 128), BF),
+            pltpu.VMEM((2, 64, 128), F32),
+            pltpu.VMEM((128, 128), jnp.int16),
+            pltpu.VMEM((8, 128), F32),
+            pltpu.VMEM((8, 128, 128), jnp.int16),
+            pltpu.VMEM((8, 8, 128), F32),
             pltpu.VMEM((2, 16, 16, 128), BF),
             dma((7,)), dma((4,)), dma((8,)), dma((8,)), dma((8,)), dma((8,)),
             dma((3,)), dma((3,)), dma((76,)), dma((76,)),
@@ -727,7 +733,6 @@
             flops=7_000_000_000, bytes_accessed=6_000_000, transcendentals=0
         ),
     )(
-        block_count,
         send_face,
         jnp.swapaxes(send_corner, 1, 2),
         features.reshape(blocks),

time: 54.2 us -> 51.3 us (0.946)
  Pallas kernels: 52.6 us -> 50.4 us
  between operations: 1.45 us -> 0.8 us
    pallas_call x1, Pallas kernels: 49.8 us -> 47.5 us  [per_device(): pl.pallas_call(body, out_shape=(jax.ShapeDtypeStruct(blocks, BF), jax.Sha...]
where the time goes in v3:
time: 51.3 us; the launch traced here: 51.2 us
  Pallas kernels  50.4 us (98%)
  between operations  0.8 us (2%)
    pallas_call x1, Pallas kernels, per_device(): pl.pallas_call(body, out_shape=(jax.ShapeDtypeStruct(blocks, BF), jax.Sha...  47.5 us
    pallas_call x1, Pallas kernels, per_device(): pl.pallas_call(finish, out_shape=(jax.ShapeDtypeStruct(blocks, BF), jax.S...  2.96 us

profile of v3, /device:TPU:1, one launch (start us, length us, event | category | flops | bytes accessed | tf_op | source)
XLA Modules:
  0.0 51.2 jit_solution(9019081056622248298)
XLA Ops:
  0.6 47.5 %shard_map.85 = (bf16[32,64,128]{2,1,0:T(8,128)(2,1)}, bf16[32,64,128]{2,1,0:T(8,128)(2,1)}, bf16[2,16,128,128]{3,2,1,0:T(8,128)(2,1)}) custom-call(s32[1,4,8]{2,1,0:T(4,128)} %face_in.1, s32[1,2,4]{2,1,0:T(2,128)} %bitcast.9, bf16[32,64,128]{2,1,0:T(8,128)(2,1)} %bitcast.5, bf16[32,64,128]{2,1,0:T(8,128)(2,1)} %bitcast.6, bf16[27,128,128]{2,1,0:T(8,128)(2,1)} %ker_in.1, ...), custom_call_target="tpu_custom_call" | custom-call | flops 7000000000 | bytes 6000000 | tf_op jit(solution)/shard_map/pallas_call | solution.py:670
  48.1 3.0 %shard_map.86 = (bf16[32,64,128]{2,1,0:T(8,128)(2,1)}, bf16[32,64,128]{2,1,0:T(8,128)(2,1)}, f32[27,128,128]{2,1,0:T(8,128)}) custom-call(bf16[32,64,128]{2,1,0:T(8,128)(2,1)} %get-tuple-element.9.conv, bf16[32,64,128]{2,1,0:T(8,128)(2,1)} %get-tuple-element.10.igrad, bf16[2,16,128,128]{3,2,1,0:T(8,128)(2,1)} %get-tuple-element.11.kg), custom_call_target="tpu_custom_call" | custom-call | tf_op jit(solution)/shard_map/pallas_call | solution.py:743

commit v4 on v3

--- a/solution.py
+++ b/solution.py
@@ -92,7 +92,7 @@
     et, pz, gz, gt, gty, wt, di, dp, de, oh, oht, bd, bdt, co, perm, pair_perm, part_perm,
     hs, hr, rs, rr,
     wd, rcore, hh, q1, r1, s1, q2, r2, qs, rscale, s2, q3, qs3, r3, rscale3, g2,
-    isem, osem, hsem, hrem, bsem, brem, csem, crem, asem, arem,
+    isem, osem, hsem, hrem, brem, csem, crem, asem, arem,
 ):
     loads = [
         pltpu.make_async_copy(src, dst, isem.at[n])
@@ -144,12 +144,6 @@
     def swap16(v):
         return nn(perm[...], v.reshape(256, 128)).reshape(16, 16, 128)
 
-    def clear(u, carry):
-        et[u, pl.ds(32, 96), :] = jnp.zeros((96, 128), BF)
-        return carry
-
-    lax.fori_loop(0, 64, clear, 0)
-
     r32, c32 = iota((32, 128), 0), iota((32, 128), 1)
     same_z = (r32 >> 3) == (c32 >> 5)
     loads[0].wait()
@@ -234,6 +228,9 @@
         gty[n, 1] = turned.astype(BF)
         gty[n, 2] = jnp.where(c256 < 192, turned, 0.0).astype(BF)
 
+    for u in range(64):
+        et[u, pl.ds(32, 48), :] = jnp.zeros((48, 128), BF)
+
     columns = c32 + jnp.where(c32 >= 32, 1, 0)
     for o in range(27):
         oh[o] = onehot(near[:, o : o + 1] == columns)
@@ -325,17 +322,33 @@
                 found = outer(readers(ux, uy, uz))
                 if found:
                     picks = stacked([r[3] for r in found])
-                    keep(nn(picks, et[ux * 16 + uy * 4 + uz]).astype(BF), found)
-
-    def send(src, dst, n, device):
-        return pltpu.make_async_remote_copy(
+                    keep(nn(picks[:, :80], et[ux * 16 + uy * 4 + uz]).astype(BF), found)
+
+    def send(src, dst, ns, nr, device):
+        pltpu.make_async_remote_copy(
             src_ref=src,
             dst_ref=dst,
-            send_sem=asem.at[n],
-            recv_sem=arem.at[n],
+            send_sem=asem.at[ns],
+            recv_sem=arem.at[nr],
             device_id=device,
             device_id_type=MESH,
+        ).start()
+
+    def counted(ref, ns, nr):
+        return pltpu.make_async_remote_copy(
+            src_ref=ref,
+            dst_ref=ref,
+            send_sem=asem.at[ns],
+            recv_sem=arem.at[nr],
+            device_id=sibling,
+            device_id_type=MESH,
         )
+
+    def arrived(ref, nr):
+        counted(ref, 0, nr).wait_recv()
+
+    def sent(ref, ns):
+        counted(ref, ns, 0).wait_send()
 
     def sixteen(first, index):
         return pl.ds(pl.multiple_of(first + 16 * index, 16), 16)
@@ -374,7 +387,6 @@
         core_sum(s)
 
     far_first = (2, 1, 3)
-    first = []
     for n in range(2):
         size = (14, 13)[n]
         for d in far_first:
@@ -383,17 +395,14 @@
             q1[n, d - 1, pl.ds(0, size)] = coded.reshape(size, 16, 128)
             qs[0, n, d - 1] = scale
             device = (along_x, along_y)[n][d - 1]
-            first.append(
-                send(
-                    q1.at[n, d - 1, pl.ds(0, size)],
-                    r1.at[n, d - 1, pl.ds(0, size)],
-                    3 * n + d - 1,
-                    device,
-                )
+            send(
+                q1.at[n, d - 1, pl.ds(0, size)],
+                r1.at[n, d - 1, pl.ds(0, size)],
+                n,
+                n,
+                (along_x, along_y)[n][d - 1],
             )
-            first.append(send(qs.at[0, n, d - 1], rscale.at[0, n, d - 1], 6 + 3 * n + d - 1, device))
-            first[-2].start()
-            first[-1].start()
+            send(qs.at[0, n, d - 1], rscale.at[0, n, d - 1], 2, 2, (along_x, along_y)[n][d - 1])
 
     def weights(j, carry):
         low, mid, high = ker[3 * j], ker[3 * j + 1], ker[3 * j + 2]
@@ -434,8 +443,9 @@
                         term = one if term is None else term + one
                 dp[px, pl.ds(ky, 4), pl.ds(w, 2)] += term.reshape(4, 2, 32, 256)
 
-    for copy in first:
-        copy.wait()
+    arrived(r1.at[0], 0)
+    arrived(r1.at[1, :, pl.ds(0, 13)], 1)
+    arrived(rscale.at[0], 2)
     for n in range(2):
         size = (14, 13)[n]
         total = hh[n, pl.ds(0, size), sixteen(0, (cx, cy)[n]), :]
@@ -445,17 +455,14 @@
         s1[n, pl.ds(0, size)] = total
         s1[n, pl.ds(size, 16 - size)] = jnp.zeros((16 - size, 16, 128), F32)
 
-    second = []
     for n in range(2):
         for d in far_first:
             coded, scale = encode(s1[n, quarter(((cy, cx)[n] + d) % 4)].reshape(64, 128))
             q2[n, d - 1] = coded.reshape(4, 16, 128)
             qs[1, n, d - 1] = scale
             device = (along_y, along_x)[n][d - 1]
-            second.append(send(q2.at[n, d - 1], r2.at[n, d - 1], 12 + 3 * n + d - 1, device))
-            second.append(send(qs.at[1, n, d - 1], rscale.at[1, n, d - 1], 18 + 3 * n + d - 1, device))
-            second[-2].start()
-            second[-1].start()
+            send(q2.at[n, d - 1], r2.at[n, d - 1], 3, 3, device)
+            send(qs.at[1, n, d - 1], rscale.at[1, n, d - 1], 4, 4, device)
 
     for ux in range(4):
         for uy in range(4):
@@ -494,7 +501,8 @@
     for ch in range(8):
         @pl.when(there[ch])
         def _():
-            halo_copy(rs, rr, bsem, brem, ch).start()
+            halo_copy(hs, hr, hsem, hrem, ch).wait_send()
+            halo_copy(rs, rr, hsem, brem, ch).start()
 
         @pl.when(jnp.logical_not(there[ch]))
         def _():
@@ -512,8 +520,8 @@
     convolve(0)
     convolve(1)
 
-    for copy in second:
-        copy.wait()
+    arrived(r2, 3)
+    arrived(rscale.at[1], 4)
     for n in range(2):
         total = s1[n, quarter((cy, cx)[n])].reshape(64, 128)
         for d in range(3):
@@ -525,12 +533,9 @@
     qs3[...] = scale
     r3[pl.ds(cz, 1)] = coded[None]
     rscale3[pl.ds(cz, 1)] = scale[None]
-    third = []
     for d in (4, 3, 5, 2, 6, 1, 7):
-        third.append(send(q3, r3.at[cz], 23 + d, along_z[d - 1]))
-        third.append(send(qs3, rscale3.at[cz], 30 + d, along_z[d - 1]))
-    for copy in third:
-        copy.start()
+        send(q3, r3.at[cz], 5, 5, along_z[d - 1])
+        send(qs3, rscale3.at[cz], 6, 6, along_z[d - 1])
 
     convolve(2)
     convolve(3)
@@ -549,7 +554,7 @@
     for ch in range(8):
         @pl.when(there[ch])
         def _():
-            halo_arrived(rs, rr, bsem, brem, ch).wait_recv()
+            halo_arrived(rs, rr, hsem, brem, ch).wait_recv()
 
     for ux in range(4):
         parts = []
@@ -570,8 +575,8 @@
     igrad_copy = pltpu.make_async_copy(igrad, igrad_out, osem.at[1])
     igrad_copy.start()
 
-    for copy in third:
-        copy.wait()
+    arrived(r3.at[pl.ds(0, 7)], 5)
+    arrived(rscale3.at[pl.ds(0, 7)], 6)
     whole = decode(r3[0], rscale3[0])
     for z in range(1, 8):
         whole = whole + decode(r3[z], rscale3[z])
@@ -580,55 +585,69 @@
     g2[1, quarter(cx)] = whole[1]
 
     def across(n, away):
-        piece = g2.at[n, quarter(((cy, cx)[n] + 4 - away) % 4)]
+        index = ((cy, cx)[n] + 4 - away) % 4
         rows = sixteen(64 * core, (cx, cy)[n])
-        copies = {}
-        for d in far_first:
-            copy = send(
-                piece,
-                kg.at[n, quarter(((cy, cx)[n] + 4 - away) % 4), rows, :],
-                44 + 12 * n + 3 * away + d - 1,
-                (along_x, along_y)[n][d - 1],
-            )
-            copy.start()
-            copies[d] = copy
-        return copies
-
-    fifth = {}
+
+        def go(slots):
+            for d in far_first:
+                send(
+                    g2.at[n, slots],
+                    kg.at[n, slots, rows, :],
+                    9 + n,
+                    11 + 2 * d + n,
+                    (along_x, along_y)[n][d - 1],
+                )
+
+        @pl.when(index < 3)
+        def _():
+            go(quarter(index))
+
+        @pl.when(index == 3)
+        def _():
+            go(pl.ds(12, (2, 1)[n]))
+
     for d in far_first:
         for n in range(2):
             piece = g2.at[n, quarter((cy, cx)[n])]
-            fifth[d, n] = send(piece, piece, 36 + 2 * d + n, (along_y, along_x)[n][d - 1])
-            fifth[d, n].start()
-    sixth = [across(n, 0) for n in range(2)]
+            send(piece, piece, 7 + n, 5 + 2 * d + n, (along_y, along_x)[n][d - 1])
+    for n in range(2):
+        across(n, 0)
     for d in (1, 3, 2):
         for n in range(2):
-            fifth[d, n].wait()
-            sixth.append(across(n, d))
-
-    last = []
+            arrived(g2.at[n, quarter(((cy, cx)[n] + 4 - d) % 4)], 5 + 2 * d + n)
+            across(n, d)
+
+    own = []
+    slots = (pl.ds(0, 14), pl.ds(0, 13))
     for n in range(2):
-        rows = sixteen(64 * core, (cx, cy)[n])
-        last.append(pltpu.make_async_copy(g2.at[n], kg.at[n, :, rows, :], osem.at[2 + n]))
-        last.append(send(g2.at[n], kg.at[n, :, rows, :], 68 + n, sibling))
-    for copy in last:
-        copy.start()
+        rows = kg.at[n, slots[n], sixteen(64 * core, (cx, cy)[n]), :]
+        own.append(pltpu.make_async_copy(g2.at[n, slots[n]], rows, osem.at[2 + n]))
+        own[n].start()
+        send(g2.at[n, slots[n]], rows, 11 + n, 19 + n, sibling)
     for d in (1, 3, 2):
         for n in range(2):
-            for group in sixth[n::2]:
-                group[d].wait()
-            rows = kg.at[n, :, sixteen(64 * core, ((cx, cy)[n] + 4 - d) % 4), :]
-            forward = send(rows, rows, 68 + 2 * d + n, sibling)
-            forward.start()
-            last.append(forward)
-    for copy in last + [conv_copy, igrad_copy]:
-        copy.wait()
-
+            rows = kg.at[n, slots[n], sixteen(64 * core, ((cx, cy)[n] + 4 - d) % 4), :]
+            arrived(rows, 11 + 2 * d + n)
+            send(rows, rows, 11 + n, 19 + n, sibling)
+
+    sent(q1.at[0], 0)
+    sent(q1.at[1, :, pl.ds(0, 13)], 1)
+    sent(qs.at[0], 2)
+    sent(q2, 3)
+    sent(qs.at[1], 4)
+    sent(r3.at[pl.ds(0, 7)], 5)
+    sent(rscale3.at[pl.ds(0, 7)], 6)
     for ch in range(8):
         @pl.when(there[ch])
         def _():
-            halo_copy(hs, hr, hsem, hrem, ch).wait_send()
-            halo_copy(rs, rr, bsem, brem, ch).wait_send()
+            halo_copy(rs, rr, hsem, brem, ch).wait_send()
+    for copy in own + [conv_copy, igrad_copy]:
+        copy.wait()
+    for n in range(2):
+        sent(g2.at[n, pl.ds(0, 12)], 7 + n)
+        sent(kg.at[n, slots[n], pl.ds(0, 48), :], 9 + n)
+        sent(kg.at[n, slots[n], pl.ds(0, 64), :], 11 + n)
+        arrived(kg.at[n, slots[n], pl.ds(other, 64), :], 19 + n)
 
 
 def finish(conv, igrad, kg, conv_out, igrad_out, kgrad_out, conv_v, igrad_v, held, wide, sem):
@@ -639,7 +658,6 @@
     loads = [pltpu.make_async_copy(*places[n], sem.at[n]) for n in range(5)]
     for n in (2, 0, 1, 3, 4):
         loads[n].start()
-    eye = onehot(iota((128, 128), 0) == iota((128, 128), 1))
     stores = []
 
     def store(src, dst):
@@ -650,7 +668,7 @@
         loads[2 + s].wait()
         for n, (matrix, slot, count) in enumerate(RUNS[s]):
             for m in range(count):
-                wide[matrix + m] = nt(eye, held[n, slot + m])
+                wide[matrix + m] = held[n, slot + m].astype(F32).T
         part = pl.ds(9 * s, 9)
         store(wide.at[part], kgrad_out.at[part])
         if s == 0:
@@ -686,7 +704,7 @@
             pltpu.VMEM((32, 128), F32),
             pltpu.VMEM(blocks, BF),
             pltpu.VMEM(blocks, BF),
-            pltpu.VMEM((64, 128, 128), BF),
+            pltpu.VMEM((64, 80, 128), BF),
             pltpu.VMEM((6, 6, 3, 32, 256), BF),
             pltpu.VMEM((4, 4, 2, 32, 256), BF),
             pltpu.VMEM((256, 1024), BF),
@@ -723,8 +741,8 @@
             pltpu.VMEM((8, 128, 128), jnp.int16),
             pltpu.VMEM((8, 8, 128), F32),
             pltpu.VMEM((2, 16, 16, 128), BF),
-            dma((7,)), dma((4,)), dma((8,)), dma((8,)), dma((8,)), dma((8,)),
-            dma((3,)), dma((3,)), dma((76,)), dma((76,)),
+            dma((6,)), dma((4,)), dma((8,)), dma((8,)), dma((8,)),
+            dma((3,)), dma((3,)), dma((13,)), dma((21,)),
         ],
         compiler_params=pltpu.CompilerParams(
             collective_id=0, has_side_effects=True, vmem_limit_bytes=62 * 1024 * 1024

time: 51.3 us -> 49.6 us (0.967)
  Pallas kernels: 50.4 us -> 48.7 us
    pallas_call x1, Pallas kernels: 47.5 us -> 45.9 us  [per_device(): pl.pallas_call(body, out_shape=(jax.ShapeDtypeStruct(blocks, BF), jax.Sha...]
where the time goes in v4:
time: 49.6 us; the launch traced here: 49.5 us
  Pallas kernels  48.7 us (98%)
  between operations  0.8 us (2%)
    pallas_call x1, Pallas kernels, per_device(): pl.pallas_call(body, out_shape=(jax.ShapeDtypeStruct(blocks, BF), jax.Sha...  45.9 us
    pallas_call x1, Pallas kernels, per_device(): pl.pallas_call(finish, out_shape=(jax.ShapeDtypeStruct(blocks, BF), jax.S...  2.78 us

profile of v4, /device:TPU:1, one launch (start us, length us, event | category | flops | bytes accessed | tf_op | source)
XLA Modules:
  0.0 49.5 jit_solution(13125181787287349970)
XLA Ops:
  0.6 45.9 %shard_map.85 = (bf16[32,64,128]{2,1,0:T(8,128)(2,1)}, bf16[32,64,128]{2,1,0:T(8,128)(2,1)}, bf16[2,16,128,128]{3,2,1,0:T(8,128)(2,1)}) custom-call(s32[1,4,8]{2,1,0:T(4,128)} %face_in.1, s32[1,2,4]{2,1,0:T(2,128)} %bitcast.9, bf16[32,64,128]{2,1,0:T(8,128)(2,1)} %bitcast.5, bf16[32,64,128]{2,1,0:T(8,128)(2,1)} %bitcast.6, bf16[27,128,128]{2,1,0:T(8,128)(2,1)} %ker_in.1, ...), custom_call_target="tpu_custom_call" | custom-call | flops 7000000000 | bytes 6000000 | tf_op jit(solution)/shard_map/pallas_call | solution.py:688
  46.5 2.8 %shard_map.86 = (bf16[32,64,128]{2,1,0:T(8,128)(2,1)}, bf16[32,64,128]{2,1,0:T(8,128)(2,1)}, f32[27,128,128]{2,1,0:T(8,128)}) custom-call(bf16[32,64,128]{2,1,0:T(8,128)(2,1)} %get-tuple-element.9.conv, bf16[32,64,128]{2,1,0:T(8,128)(2,1)} %get-tuple-element.10.igrad, bf16[2,16,128,128]{3,2,1,0:T(8,128)(2,1)} %get-tuple-element.11.kg), custom_call_target="tpu_custom_call" | custom-call | tf_op jit(solution)/shard_map/pallas_call | solution.py:761

commit v5 on v4

--- a/solution.py
+++ b/solution.py
@@ -87,8 +87,8 @@
 
 def body(
     face_in, corner_in, feat_in, cot_in, ker_in, near_in,
-    conv_out, igrad_out, kg,
-    face, corner, feat, cot, ker, near, live, conv, igrad,
+    conv, igrad, kg,
+    face, corner, feat, cot, ker, near, live,
     et, pz, gz, gt, gty, wt, di, dp, de, oh, oht, bd, bdt, co, perm, pair_perm, part_perm,
     hs, hr, rs, rr,
     wd, rcore, hh, q1, r1, s1, q2, r2, qs, rscale, s2, q3, qs3, r3, rscale3, g2,
@@ -130,9 +130,15 @@
 
     barrier = pltpu.get_barrier_semaphore()
     greet = [along_z[n] for n in (3, 2, 4, 1, 5, 0, 6)] + along_x + along_y + [sibling]
-    greet += [((gx + wx + 64) % 64, (gy + wy + 4) % 4) for wx, wy in WAYS]
+    expected = len(greet)
     for other in greet:
         pl.semaphore_signal(barrier, inc=1, device_id=other, device_id_type=MESH)
+    for ch in (4, 5, 6, 7, 0, 1, 2, 3):
+        expected = expected + there[ch].astype(jnp.int32)
+
+        @pl.when(there[ch])
+        def _():
+            pl.semaphore_signal(barrier, inc=1, device_id=halo[ch], device_id_type=MESH)
 
     r256, c256 = iota((256, 256), 0), iota((256, 256), 1)
     perm[...] = onehot(((r256 >> 4) == (c256 & 15)) & ((r256 & 15) == (c256 >> 4)))
@@ -178,7 +184,7 @@
             source = et[pl.ds(rim_base(ch, chunk), 4), pl.ds(0, 32), :].reshape(128, 128)
             hs[ch, chunk] = nn(bd[ch], source).astype(BF)
 
-    pl.semaphore_wait(barrier, len(greet))
+    pl.semaphore_wait(barrier, expected)
 
     def part(buf, ch):
         return buf.at[ch] if ch < 4 else buf.at[ch, pl.ds(0, 1)]
@@ -203,7 +209,7 @@
             device_id_type=MESH,
         )
 
-    for ch in range(8):
+    for ch in (4, 5, 6, 7, 0, 1, 2, 3):
         @pl.when(there[ch])
         def _():
             halo_copy(hs, hr, hsem, hrem, ch).start()
@@ -548,9 +554,6 @@
             rows = nn(part_perm[...], jnp.concatenate(parts, axis=0)).reshape(16, 16, 128)
             conv[pl.ds(16 * hb, 16), pl.ds(16 * x, 16), :] = rows.astype(BF)
 
-    conv_copy = pltpu.make_async_copy(conv, conv_out, osem.at[0])
-    conv_copy.start()
-
     for ch in range(8):
         @pl.when(there[ch])
         def _():
@@ -572,9 +575,6 @@
             swapped = swap16(parts[:, 16 * hb : 16 * hb + 16])
             igrad[pl.ds(16 * hb, 16), pl.ds(16 * ux, 16), :] = swapped.astype(BF)
 
-    igrad_copy = pltpu.make_async_copy(igrad, igrad_out, osem.at[1])
-    igrad_copy.start()
-
     arrived(r3.at[pl.ds(0, 7)], 5)
     arrived(rscale3.at[pl.ds(0, 7)], 6)
     whole = decode(r3[0], rscale3[0])
@@ -621,7 +621,7 @@
     slots = (pl.ds(0, 14), pl.ds(0, 13))
     for n in range(2):
         rows = kg.at[n, slots[n], sixteen(64 * core, (cx, cy)[n]), :]
-        own.append(pltpu.make_async_copy(g2.at[n, slots[n]], rows, osem.at[2 + n]))
+        own.append(pltpu.make_async_copy(g2.at[n, slots[n]], rows, osem.at[n]))
         own[n].start()
         send(g2.at[n, slots[n]], rows, 11 + n, 19 + n, sibling)
     for d in (1, 3, 2):
@@ -641,7 +641,7 @@
         @pl.when(there[ch])
         def _():
             halo_copy(rs, rr, hsem, brem, ch).wait_send()
-    for copy in own + [conv_copy, igrad_copy]:
+    for copy in own:
         copy.wait()
     for n in range(2):
         sent(g2.at[n, pl.ds(0, 12)], 7 + n)
@@ -650,32 +650,22 @@
         arrived(kg.at[n, slots[n], pl.ds(other, 64), :], 19 + n)
 
 
-def finish(conv, igrad, kg, conv_out, igrad_out, kgrad_out, conv_v, igrad_v, held, wide, sem):
-    places = [(conv, conv_v), (igrad, igrad_v)]
+def finish(conv, igrad, kg, conv_out, igrad_out, kgrad_out, wide, sem):
+    stores = []
+
+    def store(src, dst):
+        stores.append(pltpu.make_async_copy(src, dst, sem.at[len(stores)]))
+        stores[-1].start()
+
     for s in range(3):
-        slots = pl.ds(*((0, 5), (5, 5), (10, 4))[s])
-        places.append((kg.at[:, slots], held.at[:, slots]))
-    loads = [pltpu.make_async_copy(*places[n], sem.at[n]) for n in range(5)]
-    for n in (2, 0, 1, 3, 4):
-        loads[n].start()
-    stores = []
-
-    def store(src, dst):
-        stores.append(pltpu.make_async_copy(src, dst, sem.at[5 + len(stores)]))
-        stores[-1].start()
-
-    for s in range(3):
-        loads[2 + s].wait()
         for n, (matrix, slot, count) in enumerate(RUNS[s]):
             for m in range(count):
-                wide[matrix + m] = held[n, slot + m].astype(F32).T
+                wide[matrix + m] = kg[n, slot + m].T.astype(F32)
         part = pl.ds(9 * s, 9)
         store(wide.at[part], kgrad_out.at[part])
         if s == 0:
-            loads[0].wait()
-            store(conv_v, conv_out)
-            loads[1].wait()
-            store(igrad_v, igrad_out)
+            store(conv, conv_out)
+            store(igrad, igrad_out)
     for copy in stores:
         copy.wait()
 
@@ -688,12 +678,12 @@
     conv, igrad, kg = pl.pallas_call(
         body,
         out_shape=(
-            jax.ShapeDtypeStruct(blocks, BF),
-            jax.ShapeDtypeStruct(blocks, BF),
-            jax.ShapeDtypeStruct((2, 16, 128, 128), BF),
+            pltpu.VMEM(blocks, BF),
+            pltpu.VMEM(blocks, BF),
+            pltpu.VMEM((2, 16, 128, 128), BF),
         ),
         in_specs=[hbm] * 6,
-        out_specs=(hbm,) * 3,
+        out_specs=(vmem,) * 3,
         scratch_shapes=[
             pltpu.SMEM((1, 4, 8), jnp.int32),
             pltpu.SMEM((1, 2, 4), jnp.int32),
@@ -702,8 +692,6 @@
             pltpu.VMEM((27, 128, 128), BF),
             pltpu.VMEM((32, 27), jnp.int32),
             pltpu.VMEM((32, 128), F32),
-            pltpu.VMEM(blocks, BF),
-            pltpu.VMEM(blocks, BF),
             pltpu.VMEM((64, 80, 128), BF),
             pltpu.VMEM((6, 6, 3, 32, 256), BF),
             pltpu.VMEM((4, 4, 2, 32, 256), BF),
@@ -741,11 +729,11 @@
             pltpu.VMEM((8, 128, 128), jnp.int16),
             pltpu.VMEM((8, 8, 128), F32),
             pltpu.VMEM((2, 16, 16, 128), BF),
-            dma((6,)), dma((4,)), dma((8,)), dma((8,)), dma((8,)),
+            dma((6,)), dma((2,)), dma((8,)), dma((8,)), dma((8,)),
             dma((3,)), dma((3,)), dma((13,)), dma((21,)),
         ],
         compiler_params=pltpu.CompilerParams(
-            collective_id=0, has_side_effects=True, vmem_limit_bytes=62 * 1024 * 1024
+            collective_id=0, has_side_effects=True, vmem_limit_bytes=52 * 1024 * 1024
         ),
         cost_estimate=pl.CostEstimate(
             flops=7_000_000_000, bytes_accessed=6_000_000, transcendentals=0
@@ -765,16 +753,13 @@
             jax.ShapeDtypeStruct(blocks, BF),
             jax.ShapeDtypeStruct((27, 128, 128), F32),
         ),
-        in_specs=[hbm] * 3,
+        in_specs=[vmem] * 3,
         out_specs=(hbm, hbm, hbm),
         scratch_shapes=[
-            pltpu.VMEM(blocks, BF),
-            pltpu.VMEM(blocks, BF),
-            pltpu.VMEM((2, 16, 128, 128), BF),
             pltpu.VMEM((27, 128, 128), F32),
-            dma((10,)),
+            dma((5,)),
         ],
-        compiler_params=pltpu.CompilerParams(vmem_limit_bytes=62 * 1024 * 1024),
+        compiler_params=pltpu.CompilerParams(vmem_limit_bytes=32 * 1024 * 1024),
     )(conv, igrad, kg)
     return conv.reshape(2048, 128), igrad.reshape(2048, 128), kgrad
 

time: 49.6 us -> 47.8 us (0.964)
  Pallas kernels: 48.7 us -> 46.9 us
    pallas_call x1, Pallas kernels: 2.78 us -> 1.73 us  [per_device(): pl.pallas_call(finish, out_shape=(jax.ShapeDtypeStruct(blocks, BF), jax.S...]
    pallas_call x1, Pallas kernels: 45.9 us -> 45.2 us  [per_device(): pl.pallas_call(body, out_shape=(pltpu.VMEM(blocks, BF), pltpu.VMEM(blocks...]
where the time goes in v5:
time: 47.8 us; the launch traced here: 47.7 us
  Pallas kernels  46.9 us (98%)
  between operations  0.8 us (2%)
    pallas_call x1, Pallas kernels, per_device(): pl.pallas_call(body, out_shape=(pltpu.VMEM(blocks, BF), pltpu.VMEM(blocks...  45.2 us
    pallas_call x1, Pallas kernels, per_device(): pl.pallas_call(finish, out_shape=(jax.ShapeDtypeStruct(blocks, BF), jax.S...  1.73 us

profile of v5, /device:TPU:1, one launch (start us, length us, event | category | flops | bytes accessed | tf_op | source)
XLA Modules:
  0.0 47.7 jit_solution(2071986988705505006)
XLA Ops:
  0.6 45.2 %shard_map.85 = (bf16[32,64,128]{2,1,0:T(8,128)(2,1)S(1)}, bf16[32,64,128]{2,1,0:T(8,128)(2,1)S(1)}, bf16[2,16,128,128]{3,2,1,0:T(8,128)(2,1)S(1)}) custom-call(s32[1,4,8]{2,1,0:T(4,128)} %face_in.1, s32[1,2,4]{2,1,0:T(2,128)} %bitcast.9, bf16[32,64,128]{2,1,0:T(8,128)(2,1)} %bitcast.5, bf16[32,64,128]{2,1,0:T(8,128)(2,1)} %bitcast.6, ...), custom_call_target="tpu_custom_call" | custom-call | flops 7000000000 | bytes 6000000 | tf_op jit(solution)/shard_map/pallas_call | solution.py:678
  45.8 1.7 %shard_map.86 = (bf16[32,64,128]{2,1,0:T(8,128)(2,1)}, bf16[32,64,128]{2,1,0:T(8,128)(2,1)}, f32[27,128,128]{2,1,0:T(8,128)}) custom-call(bf16[32,64,128]{2,1,0:T(8,128)(2,1)S(1)} %get-tuple-element.9.conv, bf16[32,64,128]{2,1,0:T(8,128)(2,1)S(1)} %get-tuple-element.10.igrad, bf16[2,16,128,128]{3,2,1,0:T(8,128)(2,1)S(1)} %get-tuple-element.11.kg), custom_call_target="tpu_custom_call" | custom-call | tf_op jit(solution)/shard_map/pallas_call | solution.py:749

commit v6 on v5

--- a/solution.py
+++ b/solution.py
@@ -209,7 +209,7 @@
             device_id_type=MESH,
         )
 
-    for ch in (4, 5, 6, 7, 0, 1, 2, 3):
+    for ch in (2, 3, 4, 5, 6, 7, 0, 1):
         @pl.when(there[ch])
         def _():
             halo_copy(hs, hr, hsem, hrem, ch).start()
@@ -253,8 +253,20 @@
     def inner(found):
         return [r for r in found if 1 <= r[0] <= 4 and 1 <= r[1] <= 4]
 
-    def outer(found):
-        return [r for r in found if not (1 <= r[0] <= 4 and 1 <= r[1] <= 4)]
+    def outer_y(found):
+        return [r for r in found if 1 <= r[0] <= 4 and not 1 <= r[1] <= 4]
+
+    def outer_x(found):
+        return [r for r in found if not 1 <= r[0] <= 4]
+
+    def gather(which):
+        for ux in range(4):
+            for uy in range(4):
+                for uz in range(4):
+                    found = which(readers(ux, uy, uz))
+                    if found:
+                        picks = stacked([r[3] for r in found])[:, :80]
+                        keep(nn(picks, et[ux * 16 + uy * 4 + uz]).astype(BF), found)
 
     def keep(rows, found):
         for n, (px, py, p, _) in enumerate(found):
@@ -306,7 +318,7 @@
                 else:
                     di[9 * kx + 3 * ky + n] = value
 
-    for ch in range(8):
+    def unpack(ch):
         @pl.when(there[ch])
         def _():
             halo_arrived(hs, hr, hsem, hrem, ch).wait_recv()
@@ -322,14 +334,6 @@
                     pair, axis=1
                 ).astype(BF)
 
-    for ux in range(4):
-        for uy in range(4):
-            for uz in range(4):
-                found = outer(readers(ux, uy, uz))
-                if found:
-                    picks = stacked([r[3] for r in found])
-                    keep(nn(picks[:, :80], et[ux * 16 + uy * 4 + uz]).astype(BF), found)
-
     def send(src, dst, ns, nr, device):
         pltpu.make_async_remote_copy(
             src_ref=src,
@@ -380,7 +384,7 @@
             total = term if total is None else total + term
         return total
 
-    for s in (1, 0, 2):
+    def outer_wgrad(s):
         for ky in range(3):
             if s == 1 and ky == 1:
                 continue
@@ -389,6 +393,16 @@
                 j = 9 * s + 3 * ky + n
                 wd[j] = di[j] + value[n]
         core_copy(s).start()
+
+    for ch in (2, 3):
+        unpack(ch)
+    gather(outer_y)
+    outer_wgrad(1)
+    for ch in (4, 5, 6, 7, 0, 1):
+        unpack(ch)
+    gather(outer_x)
+    outer_wgrad(0)
+    outer_wgrad(2)
     for s in (1, 0, 2):
         core_sum(s)
 
@@ -657,15 +671,14 @@
         stores.append(pltpu.make_async_copy(src, dst, sem.at[len(stores)]))
         stores[-1].start()
 
+    store(conv, conv_out)
+    store(igrad, igrad_out)
     for s in range(3):
         for n, (matrix, slot, count) in enumerate(RUNS[s]):
             for m in range(count):
                 wide[matrix + m] = kg[n, slot + m].T.astype(F32)
         part = pl.ds(9 * s, 9)
         store(wide.at[part], kgrad_out.at[part])
-        if s == 0:
-            store(conv, conv_out)
-            store(igrad, igrad_out)
     for copy in stores:
         copy.wait()
 

time: 47.8 us -> 46.6 us (0.975)
  Pallas kernels: 46.9 us -> 45.7 us
    pallas_call x1, Pallas kernels: 45.2 us -> 44.1 us  [per_device(): pl.pallas_call(body, out_shape=(pltpu.VMEM(blocks, BF), pltpu.VMEM(blocks...]
where the time goes in v6:
time: 46.6 us; the launch traced here: 46.5 us
  Pallas kernels  45.7 us (98%)
  between operations  0.8 us (2%)
    pallas_call x1, Pallas kernels, per_device(): pl.pallas_call(body, out_shape=(pltpu.VMEM(blocks, BF), pltpu.VMEM(blocks...  44.1 us
    pallas_call x1, Pallas kernels, per_device(): pl.pallas_call(finish, out_shape=(jax.ShapeDtypeStruct(blocks, BF), jax.S...  1.59 us

profile of v6, /device:TPU:1, one launch (start us, length us, event | category | flops | bytes accessed | tf_op | source)
XLA Modules:
  0.0 46.5 jit_solution(16398284007886917368)
XLA Ops:
  0.6 44.1 %shard_map.85 = (bf16[32,64,128]{2,1,0:T(8,128)(2,1)S(1)}, bf16[32,64,128]{2,1,0:T(8,128)(2,1)S(1)}, bf16[2,16,128,128]{3,2,1,0:T(8,128)(2,1)S(1)}) custom-call(s32[1,4,8]{2,1,0:T(4,128)} %face_in.1, s32[1,2,4]{2,1,0:T(2,128)} %bitcast.9, bf16[32,64,128]{2,1,0:T(8,128)(2,1)} %bitcast.5, bf16[32,64,128]{2,1,0:T(8,128)(2,1)} %bitcast.6, ...), custom_call_target="tpu_custom_call" | custom-call | flops 7000000000 | bytes 6000000 | tf_op jit(solution)/shard_map/pallas_call | solution.py:691
  44.7 1.6 %shard_map.86 = (bf16[32,64,128]{2,1,0:T(8,128)(2,1)}, bf16[32,64,128]{2,1,0:T(8,128)(2,1)}, f32[27,128,128]{2,1,0:T(8,128)}) custom-call(bf16[32,64,128]{2,1,0:T(8,128)(2,1)S(1)} %get-tuple-element.9.conv, bf16[32,64,128]{2,1,0:T(8,128)(2,1)S(1)} %get-tuple-element.10.igrad, bf16[2,16,128,128]{3,2,1,0:T(8,128)(2,1)S(1)} %get-tuple-element.11.kg), custom_call_target="tpu_custom_call" | custom-call | tf_op jit(solution)/shard_map/pallas_call | solution.py:762

commit v7 on v6

--- a/solution.py
+++ b/solution.py
@@ -422,7 +422,7 @@
                 n,
                 (along_x, along_y)[n][d - 1],
             )
-            send(qs.at[0, n, d - 1], rscale.at[0, n, d - 1], 2, 2, (along_x, along_y)[n][d - 1])
+            send(qs.at[0, n, d - 1], rscale.at[0, n, d - 1], 2, (2, 21)[n], (along_x, along_y)[n][d - 1])
 
     def weights(j, carry):
         low, mid, high = ker[3 * j], ker[3 * j + 1], ker[3 * j + 2]
@@ -463,19 +463,16 @@
                         term = one if term is None else term + one
                 dp[px, pl.ds(ky, 4), pl.ds(w, 2)] += term.reshape(4, 2, 32, 256)
 
-    arrived(r1.at[0], 0)
-    arrived(r1.at[1, :, pl.ds(0, 13)], 1)
-    arrived(rscale.at[0], 2)
     for n in range(2):
         size = (14, 13)[n]
+        arrived(r1.at[n, :, pl.ds(0, size)], n)
+        arrived(rscale.at[0, n], (2, 21)[n])
         total = hh[n, pl.ds(0, size), sixteen(0, (cx, cy)[n]), :]
         for d in range(3):
             got = decode(r1[n, d, pl.ds(0, size)].reshape(-1, 128), rscale[0, n, d])
             total = total + got.reshape(size, 16, 128)
         s1[n, pl.ds(0, size)] = total
         s1[n, pl.ds(size, 16 - size)] = jnp.zeros((16 - size, 16, 128), F32)
-
-    for n in range(2):
         for d in far_first:
             coded, scale = encode(s1[n, quarter(((cy, cx)[n] + d) % 4)].reshape(64, 128))
             q2[n, d - 1] = coded.reshape(4, 16, 128)
@@ -743,7 +740,7 @@
             pltpu.VMEM((8, 8, 128), F32),
             pltpu.VMEM((2, 16, 16, 128), BF),
             dma((6,)), dma((2,)), dma((8,)), dma((8,)), dma((8,)),
-            dma((3,)), dma((3,)), dma((13,)), dma((21,)),
+            dma((3,)), dma((3,)), dma((13,)), dma((22,)),
         ],
         compiler_params=pltpu.CompilerParams(
             collective_id=0, has_side_effects=True, vmem_limit_bytes=52 * 1024 * 1024

time: 46.6 us -> 46.5 us (level)
  no operation moved by 1% of the time
where the time goes in v7:
time: 46.5 us; the launch traced here: 46.4 us
  Pallas kernels  45.6 us (98%)
  between operations  0.8 us (2%)
    pallas_call x1, Pallas kernels, per_device(): pl.pallas_call(body, out_shape=(pltpu.VMEM(blocks, BF), pltpu.VMEM(blocks...  44.1 us
    pallas_call x1, Pallas kernels, per_device(): pl.pallas_call(finish, out_shape=(jax.ShapeDtypeStruct(blocks, BF), jax.S...  1.59 us

profile of v7, /device:TPU:1, one launch (start us, length us, event | category | flops | bytes accessed | tf_op | source)
XLA Modules:
  0.0 46.4 jit_solution(9417611315775635628)
XLA Ops:
  0.6 44.1 %shard_map.85 = (bf16[32,64,128]{2,1,0:T(8,128)(2,1)S(1)}, bf16[32,64,128]{2,1,0:T(8,128)(2,1)S(1)}, bf16[2,16,128,128]{3,2,1,0:T(8,128)(2,1)S(1)}) custom-call(s32[1,4,8]{2,1,0:T(4,128)} %face_in.1, s32[1,2,4]{2,1,0:T(2,128)} %bitcast.9, bf16[32,64,128]{2,1,0:T(8,128)(2,1)} %bitcast.5, bf16[32,64,128]{2,1,0:T(8,128)(2,1)} %bitcast.6, ...), custom_call_target="tpu_custom_call" | custom-call | flops 7000000000 | bytes 6000000 | tf_op jit(solution)/shard_map/pallas_call | solution.py:688
  44.7 1.6 %shard_map.86 = (bf16[32,64,128]{2,1,0:T(8,128)(2,1)}, bf16[32,64,128]{2,1,0:T(8,128)(2,1)}, f32[27,128,128]{2,1,0:T(8,128)}) custom-call(bf16[32,64,128]{2,1,0:T(8,128)(2,1)S(1)} %get-tuple-element.9.conv, bf16[32,64,128]{2,1,0:T(8,128)(2,1)S(1)} %get-tuple-element.10.igrad, bf16[2,16,128,128]{3,2,1,0:T(8,128)(2,1)S(1)} %get-tuple-element.11.kg), custom_call_target="tpu_custom_call" | custom-call | tf_op jit(solution)/shard_map/pallas_call | solution.py:759
